TPU v7x, 32 devices: a whole 2x2x4 slice. The times are simulated.
32 devices in a mesh: groups: 1, seq: 32 (over z, y, x, core).
Axes of the slice: x: 2, y: 2, z: 4, core: 2. Of those that a mesh axis runs over, the one named last changes fastest.
Arguments:
- queries: bfloat16 [8192, 1280], P(('groups', 'seq')), may hold values from -8 to 8
- key_rows: bfloat16 [8192, 1280], P(('groups', 'seq')), may hold values from -8 to 8
- value_rows: bfloat16 [8192, 1280], P(('groups', 'seq')), may hold values from -8 to 8
- step_rates: float32 [2, 8192], P(None, ('groups', 'seq')), may hold values from 0.02 to 0.2
- fast_weights: float32 [3, 1280, 640], P(None, 'seq'), may hold values from -0.25 to 0.25
- momentum: float32 [3, 1280, 640], P('groups', 'seq'), may hold values from -0.18 to 0.18
- out_gain: float32 [1280], replicated, may hold values from 0.5 to 1.5
Outputs:
- layer_out: bfloat16 [8192, 1280], P(('groups', 'seq'))
- new_weights: float32 [3, 1280, 640], P('groups', 'seq')
- new_momentum: float32 [3, 1280, 640], P('groups', 'seq')
All inputs are finite; a program needn't handle non-finite values.
Results may differ from a plain program's by a relative error of at most 0.0089.
Values may be sent and summed in bfloat16 or wider, within the bound.
A program may use at most 128 MiB of HBM per device.

v0:
```python
import math

import jax
import jax.numpy as jnp
from jax import lax
from jax.sharding import PartitionSpec as P

FAST_HIDDEN = 640
ATT_DIM = 128
WINDOW = 1024
ATT_HEADS = 10


def from_behind(block, axis, distance):
    devices = range(lax.axis_size(axis))
    route = [(i - distance, i) for i in devices if i - distance in devices]
    return lax.ppermute(block, axis, route)


def silu_slope(values_in):
    sigmoid_val = jax.nn.sigmoid(values_in)
    return sigmoid_val * (1.0 + values_in * (1.0 - sigmoid_val))


def row_product(left_side, right_side):
    return lax.dot_general(
        left_side, right_side, (((1,), (1,)), ((), ())), preferred_element_type=jnp.float32
    )


def token_product(left_side, right_side):
    return lax.dot_general(
        left_side, right_side, (((0,), (0,)), ((), ())), preferred_element_type=jnp.float32
    )


def per_device(queries, key_rows, value_rows, step_rates, fast_weights, momentum, out_gain):
    local_tokens = queries.shape[0]
    head_count = step_rates.shape[0]
    head_dim = fast_weights.shape[2]
    owned_rows = fast_weights.shape[1]
    total_tokens = local_tokens * lax.axis_size("seq")
    grad_scale = 1.0 / math.sqrt(total_tokens)
    start_rows = lax.all_gather(fast_weights.astype(jnp.bfloat16), "seq", axis=1, tiled=True)
    key_parts = []
    out_parts = []
    hidden_parts = []
    gate_parts = []
    up_parts = []
    for head_idx in range(head_count):
        col_lo = head_idx * head_dim
        row_lo = head_idx * FAST_HIDDEN
        key_head = key_rows[:, col_lo : col_lo + head_dim]
        value_head = value_rows[:, col_lo : col_lo + head_dim]
        key_gate = row_product(key_head, start_rows[0, row_lo : row_lo + FAST_HIDDEN])
        key_up = row_product(key_head, start_rows[1, row_lo : row_lo + FAST_HIDDEN])
        key_hidden = (jax.nn.silu(key_gate) * key_up).astype(jnp.bfloat16)
        out_grad = (
            -grad_scale * step_rates[head_idx][:, None] * value_head.astype(jnp.float32)
        ).astype(jnp.bfloat16)
        key_parts.append(key_head)
        out_parts.append(out_grad)
        hidden_parts.append(key_hidden)
        hidden_grad = row_product(out_grad, start_rows[2, row_lo : row_lo + FAST_HIDDEN])
        gate_parts.append((hidden_grad * key_up * silu_slope(key_gate)).astype(jnp.bfloat16))
        up_parts.append((hidden_grad * jax.nn.silu(key_gate)).astype(jnp.bfloat16))
    gate_all = jnp.concatenate(gate_parts, axis=1)
    up_all = jnp.concatenate(up_parts, axis=1)
    hidden_all = jnp.concatenate(hidden_parts, axis=1)
    head_of = jnp.arange(lax.axis_size("seq") * owned_rows, dtype=jnp.int32) // FAST_HIDDEN
    total = jnp.zeros((lax.axis_size("seq") * owned_rows, 3, head_dim), jnp.float32)
    for owner_head_idx in range(head_count):
        block = jnp.stack(
            [
                token_product(gate_all, key_parts[owner_head_idx]),
                token_product(up_all, key_parts[owner_head_idx]),
                token_product(hidden_all, out_parts[owner_head_idx]),
            ],
            axis=1,
        )
        total = jnp.where((head_of == owner_head_idx)[:, None, None], block, total)
    owner_sum = lax.psum_scatter(total, "seq", scatter_dimension=0, tiled=True)
    grad_rows = jnp.transpose(owner_sum, (1, 0, 2))
    new_momentum = 0.9 * momentum + grad_rows
    moved_rows = fast_weights - new_momentum
    keep_norm = jnp.sqrt(jnp.mean(fast_weights * fast_weights, axis=-1, keepdims=True))
    new_weights = (
        moved_rows
        * keep_norm
        * lax.rsqrt(jnp.mean(moved_rows * moved_rows, axis=-1, keepdims=True) + 1e-06)
    )
    applied = lax.all_gather(new_weights.astype(jnp.bfloat16), "seq", axis=1, tiled=True)
    fast_list = []
    for head_idx in range(head_count):
        col_lo = head_idx * head_dim
        row_lo = head_idx * FAST_HIDDEN
        query_head = queries[:, col_lo : col_lo + head_dim]
        query_gate = row_product(query_head, applied[0, row_lo : row_lo + FAST_HIDDEN])
        query_up = row_product(query_head, applied[1, row_lo : row_lo + FAST_HIDDEN])
        query_hidden = (jax.nn.silu(query_gate) * query_up).astype(jnp.bfloat16)
        fast_out = jnp.dot(
            query_hidden,
            applied[2, row_lo : row_lo + FAST_HIDDEN],
            preferred_element_type=jnp.float32,
        )
        fast_normed = (
            fast_out
            * lax.rsqrt(jnp.mean(fast_out * fast_out, axis=-1, keepdims=True) + 1e-06)
            * out_gain[col_lo : col_lo + head_dim]
        )
        fast_list.append(fast_normed)
    fast_all = jnp.concatenate(fast_list, axis=1)
    reach_hops = WINDOW // local_tokens
    key_blocks = [None] * reach_hops
    value_blocks = [None] * reach_hops
    for hop_idx in range(1, reach_hops + 1):
        arrived = from_behind((key_rows, value_rows), "seq", hop_idx)
        key_blocks[reach_hops - hop_idx] = arrived[0]
        value_blocks[reach_hops - hop_idx] = arrived[1]
    window_keys = jnp.concatenate(key_blocks + [key_rows], axis=0)
    window_values = jnp.concatenate(value_blocks + [value_rows], axis=0)
    key_count = (reach_hops + 1) * local_tokens
    offset = lax.axis_index("seq") * local_tokens
    query_pos = offset + jnp.arange(local_tokens, dtype=jnp.int32)
    key_pos = offset - reach_hops * local_tokens + jnp.arange(key_count, dtype=jnp.int32)
    allowed = (
        (key_pos[None, :] <= query_pos[:, None])
        & (key_pos[None, :] > query_pos[:, None] - WINDOW)
        & (key_pos[None, :] >= 0)
    )
    query_heads = queries.reshape(local_tokens, ATT_HEADS, ATT_DIM)
    key_heads = window_keys.reshape(key_count, ATT_HEADS, ATT_DIM)
    value_heads = window_values.reshape(key_count, ATT_HEADS, ATT_DIM)

    def one_group(group_idx):
        q_part = lax.dynamic_slice_in_dim(query_heads, group_idx * 2, 2, 1)
        k_part = lax.dynamic_slice_in_dim(key_heads, group_idx * 2, 2, 1)
        v_part = lax.dynamic_slice_in_dim(value_heads, group_idx * 2, 2, 1)
        scores = jnp.einsum(
            "qhd,khd->hqk", q_part, k_part, preferred_element_type=jnp.float32
        ) / math.sqrt(ATT_DIM)
        scores = jnp.where(allowed[None], scores, -jnp.inf)
        top_score = jnp.max(scores, axis=-1, keepdims=True)
        exp_scores = jnp.exp(scores - top_score)
        att_probs = (exp_scores / jnp.sum(exp_scores, axis=-1, keepdims=True)).astype(jnp.bfloat16)
        attended = jnp.einsum("hqk,khd->qhd", att_probs, v_part, preferred_element_type=jnp.float32)
        return attended * lax.rsqrt(jnp.mean(attended * attended, axis=-1, keepdims=True) + 1e-06)

    att_groups = lax.map(one_group, jnp.arange(ATT_HEADS // 2, dtype=jnp.int32))
    att_all = jnp.transpose(att_groups, (1, 0, 2, 3)).reshape(local_tokens, ATT_HEADS * ATT_DIM)
    layer_out = (fast_all + att_all).astype(jnp.bfloat16)
    return (layer_out, new_weights, new_momentum)


def solution(mesh):
    placed = (
        P(("groups", "seq"), None),
        P(("groups", "seq"), None),
        P(("groups", "seq"), None),
        P(None, ("groups", "seq")),
        P(None, "seq", None),
        P("groups", "seq", None),
        P(),
    )
    return jax.shard_map(
        per_device,
        mesh=mesh,
        in_specs=placed,
        out_specs=(P(("groups", "seq"), None), P("groups", "seq", None), P("groups", "seq", None)),
        check_vma=False,
    )
```

profile of v0, /device:TPU:1, one launch (start us, length us, event | category | flops | bytes accessed | tf_op | source)
XLA Modules:
  0.0 366.1 jit_solution(3308324943723052174)
XLA Ops:
  9.7 68.8 %all-gather.3.cloned.1.call-done = bf16[3,1280,640]{2,1,0:T(8,128)(2,1)} async-done(((bf16[3,40,640]{2,1,0:T(8,128)(2,1)}), bf16[3,1280,640]{2,1,0:T(8,128)(2,1)}) %all-gather.3.cloned.1.call-update) | async-done | bytes 4915216 | tf_op jit(solution)/shard_map/all_gather | solution.py:44
  78.5 1.9 fusion.51
  80.3 1.8 fusion.48
  82.1 1.8 fusion.52
  93.0 4.8 %maximum_select_fusion = f32[1280,3,640]{2,0,1:T(8,128)} fusion(f32[1280,1,640]{2,0,1:T(8,128)S(1)} %convolution_bitcast_fusion.3, f32[1280,1,640]{2,0,1:T(8,128)S(1)} %convolution_bitcast_fusion.4, f32[1280,1,640]{2,0,1:T(8,128)S(1)} %convolution_bitcast_fusion.5, f32[1280,1,640]{2,0,1:T(8,128)S(1)} %convolution_bitcast_fusion, ...), kind=kLoop, calls=%fused_computation.25 | loop fusion | flops 14745600 | bytes 29493760 | tf_op jit(solution)/shard_map/jit(_where)/select_n | solution.py:81
  99.0 3.9 %collective-permute-start.4 = (bf16[256,1280]{0,1:T(8,128)(2,1)}, bf16[256,1280]{0,1:T(8,128)(2,1)}, u32[]{:S(2)}, u32[]{:S(2)}) collective-permute-start(bf16[256,1280]{0,1:T(8,128)(2,1)} %copy.18), channel_id=1, source_target_pairs={{0,4},{1,5},{2,6},{3,7},{4,8},{5,9},{6,10},{7,11},{8,12},{9,13},{1... | collective-permute-start | bytes 1966088 | tf_op jit(solution)/shard_map/ppermute | solution.py:17
  102.9 3.9 %collective-permute-start.5 = (bf16[256,1280]{0,1:T(8,128)(2,1)}, bf16[256,1280]{0,1:T(8,128)(2,1)}, u32[]{:S(2)}, u32[]{:S(2)}) collective-permute-start(bf16[256,1280]{0,1:T(8,128)(2,1)} %copy.18), channel_id=1, source_target_pairs={{0,3},{1,4},{2,5},{3,6},{4,7},{5,8},{6,9},{7,10},{8,11},{9,12},{10... | collective-permute-start | bytes 1966088 | tf_op jit(solution)/shard_map/ppermute | solution.py:17
  106.8 2.3 collective-permute-start
  109.2 3.1 collective-permute-start.1
  112.3 3.3 collective-permute-start.2
  115.7 155.0 %reduce-scatter.2.cloned.1.call-done = f32[40,3,640]{2,0,1:T(8,128)} async-done(((f32[1280,3,640]{2,0,1:T(8,128)}), f32[40,3,640]{2,0,1:T(8,128)}) %reduce-scatter.2.cloned.1.call-update) | async-done | bytes 307216 | tf_op jit(solution)/shard_map/reduce_scatter | solution.py:82
  274.9 1.9 collective-permute-start.3
  277.9 2.2 collective-permute-start.6
  281.3 2.1 collective-permute-start.7
  284.5 2.9 collective-permute-done.3
  288.6 3.4 copy.16
  294.5 5.3 %collective-permute-done.6 = bf16[256,1280]{0,1:T(8,128)(2,1)} collective-permute-done((bf16[256,1280]{0,1:T(8,128)(2,1)}, bf16[256,1280]{0,1:T(8,128)(2,1)}, u32[]{:S(2)}, u32[]{:S(2)}) %collective-permute-start.6) | collective-permute-done | bytes 655392 | tf_op jit(solution)/shard_map/ppermute | solution.py:17
  300.9 10.1 %collective-permute-done.7 = bf16[256,1280]{0,1:T(8,128)(2,1)} collective-permute-done((bf16[256,1280]{0,1:T(8,128)(2,1)}, bf16[256,1280]{0,1:T(8,128)(2,1)}, u32[]{:S(2)}, u32[]{:S(2)}) %collective-permute-start.7) | collective-permute-done | bytes 655392 | tf_op jit(solution)/shard_map/ppermute | solution.py:17
  315.1 34.0 %while.11 = (s32[]{:T(128)}, f32[5,256,2,128]{1,3,2,0:T(8,128)S(1)}, s32[5]{0:T(128)S(1)}, bf16[1280,10,128]{0,2,1:T(8,128)(2,1)}, bf16[256,10,128]{0,2,1:T(8,12...) while((s32[]{:T(128)}, ...), condition=%wide.region_9.10_spmd.clone, body=%wide.region_5.9_spmd.clone.sunk | while | flops 510725632 | bytes 4021187 | solution.py:149
  316.7 2.3 fusion.116
  319.0 2.8 multiply_reduce_fusion.6
  323.5 2.3 fusion.116
  325.8 2.8 multiply_reduce_fusion.6
  330.3 2.3 fusion.116
  332.6 2.8 multiply_reduce_fusion.6
  337.1 2.3 fusion.116
  339.4 2.8 multiply_reduce_fusion.6
  343.9 2.3 fusion.116
  346.2 2.8 multiply_reduce_fusion.6
  351.1 2.3 multiply_reduce_fusion.2
  353.4 2.4 convolution_bitcast_fusion.7
  355.8 2.5 multiply_reduce_fusion.1
  (95 shorter events, 37.2 us)
Async XLA Ops:
  7.2 71.3 %all-gather.3.cloned.1.call-start = ((), (), s32[]{:S(2)}) async-start(), calls=%async_computation.1 | async-start | bytes 5068800 | tf_op jit(solution)/shard_map/all_gather | solution.py:44
  8.9 261.8 %reduce-scatter.2.cloned.1.call-start = ((), (), s32[]{:S(2)}) async-start(), calls=%async_computation.2 | async-start | bytes 10137600 | tf_op jit(solution)/shard_map/reduce_scatter | solution.py:82
  78.5 5.4 %copy-start.7 = (bf16[3,1280,640]{2,1,0:T(8,128)(2,1)S(1)}, bf16[3,1280,640]{2,1,0:T(8,128)(2,1)}, u32[]{:S(2)}) copy-start(bf16[3,1280,640]{2,1,0:T(8,128)(2,1)} %all-gather.3.cloned.1.call-done) | copy-start | bytes 14745604
  80.3 5.1 %copy-start = (bf16[256,1280]{1,0:T(8,128)(2,1)S(1)}, bf16[256,1280]{1,0:T(8,128)(2,1)}, u32[]{:S(2)}) copy-start(bf16[256,1280]{1,0:T(8,128)(2,1)} %param.10) | copy-start | bytes 1966084
  97.8 17.8 %copy-start.10 = (f32[1280]{0:T(1024)S(1)}, f32[1280]{0:T(1024)}, u32[]{:S(2)}) copy-start(f32[1280]{0:T(1024)} %param.15) | copy-start | bytes 15364
  97.8 172.9 %copy-start.1 = (f32[3,40,640]{2,1,0:T(8,128)S(1)}, f32[3,40,640]{2,1,0:T(8,128)}, u32[]{:S(2)}) copy-start(f32[3,40,640]{2,1,0:T(8,128)} %param.13) | copy-start | bytes 921604
  97.8 172.9 %copy-start.8 = (f32[3,40,640]{2,1,0:T(8,128)S(1)}, f32[3,40,640]{2,1,0:T(8,128)}, u32[]{:S(2)}) copy-start(f32[3,40,640]{2,1,0:T(8,128)} %param.14) | copy-start | bytes 921604
  97.8 175.1 %copy-start.4 = (bf16[256,1280]{1,0:T(8,128)(2,1)S(1)}, bf16[256,1280]{1,0:T(8,128)(2,1)}, u32[]{:S(2)}) copy-start(bf16[256,1280]{1,0:T(8,128)(2,1)} %param.9) | copy-start | bytes 1966084
  97.8 251.6 %all-gather.5.cloned.1.call-start = ((), (), s32[]{:S(2)}) async-start(), calls=%async_computation.3 | async-start | bytes 5068800 | tf_op jit(solution)/shard_map/all_gather | solution.py:92
  99.0 193.1 %collective-permute-start.4 = (bf16[256,1280]{0,1:T(8,128)(2,1)}, bf16[256,1280]{0,1:T(8,128)(2,1)}, u32[]{:S(2)}, u32[]{:S(2)}) collective-permute-start(bf16[256,1280]{0,1:T(8,128)(2,1)} %copy.18), channel_id=1, source_target_pairs={{0,4},{1,5},{2,6},{3,7},{4,8},{5,9},{6,10},{7,11},{8,12},{9,13},{1... | collective-permute-start | bytes 1966088 | tf_op jit(solution)/shard_map/ppermute | solution.py:17
  102.9 190.4 %collective-permute-start.5 = (bf16[256,1280]{0,1:T(8,128)(2,1)}, bf16[256,1280]{0,1:T(8,128)(2,1)}, u32[]{:S(2)}, u32[]{:S(2)}) collective-permute-start(bf16[256,1280]{0,1:T(8,128)(2,1)} %copy.18), channel_id=1, source_target_pairs={{0,3},{1,4},{2,5},{3,6},{4,7},{5,8},{6,9},{7,10},{8,11},{9,12},{10... | collective-permute-start | bytes 1966088 | tf_op jit(solution)/shard_map/ppermute | solution.py:17
  106.8 167.2 %collective-permute-start = (bf16[256,1280]{1,0:T(8,128)(2,1)}, bf16[256,1280]{1,0:T(8,128)(2,1)S(1)}, u32[]{:S(2)}, u32[]{:S(2)}) collective-permute-start(bf16[256,1280]{1,0:T(8,128)(2,1)} %param.11), channel_id=1, source_target_pairs={{0,4},{1,5},{2,6},{3,7},{4,8},{5,9},{6,10},{7,11},{8,12},{9,13},{1... | collective-permute-start | bytes 1966088 | tf_op jit(solution)/shard_map/ppermute | solution.py:17
  109.2 168.8 %collective-permute-start.1 = (bf16[256,1280]{1,0:T(8,128)(2,1)}, bf16[256,1280]{1,0:T(8,128)(2,1)}, u32[]{:S(2)}, u32[]{:S(2)}) collective-permute-start(bf16[256,1280]{1,0:T(8,128)(2,1)} %param.11), channel_id=1, source_target_pairs={{0,3},{1,4},{2,5},{3,6},{4,7},{5,8},{6,9},{7,10},{8,11},{9,12},{10... | collective-permute-start | bytes 1966088 | tf_op jit(solution)/shard_map/ppermute | solution.py:17
  112.3 169.0 %collective-permute-start.2 = (bf16[256,1280]{1,0:T(8,128)(2,1)}, bf16[256,1280]{1,0:T(8,128)(2,1)}, u32[]{:S(2)}, u32[]{:S(2)}) collective-permute-start(bf16[256,1280]{1,0:T(8,128)(2,1)} %param.11), channel_id=1, source_target_pairs={{0,2},{1,3},{2,4},{3,5},{4,6},{5,7},{6,8},{7,9},{8,10},{9,11},{10,... | collective-permute-start | bytes 1966088 | tf_op jit(solution)/shard_map/ppermute | solution.py:17
  271.8 1.0 copy-start.3
  274.0 0.8 copy-start.6
  274.9 12.6 %collective-permute-start.3 = (bf16[256,1280]{1,0:T(8,128)(2,1)}, bf16[256,1280]{1,0:T(8,128)(2,1)S(1)}, u32[]{:S(2)}, u32[]{:S(2)}) collective-permute-start(bf16[256,1280]{1,0:T(8,128)(2,1)} %param.11), channel_id=1, source_target_pairs={{0,1},{1,2},{2,3},{3,4},{4,5},{5,6},{6,7},{7,8},{8,9},{9,10},{10,1... | collective-permute-start | bytes 1966088 | tf_op jit(solution)/shard_map/ppermute | solution.py:17
  277.9 21.8 %collective-permute-start.6 = (bf16[256,1280]{0,1:T(8,128)(2,1)}, bf16[256,1280]{0,1:T(8,128)(2,1)}, u32[]{:S(2)}, u32[]{:S(2)}) collective-permute-start(bf16[256,1280]{0,1:T(8,128)(2,1)} %copy.18), channel_id=1, source_target_pairs={{0,2},{1,3},{2,4},{3,5},{4,6},{5,7},{6,8},{7,9},{8,10},{9,11},{10,... | collective-permute-start | bytes 1966088 | tf_op jit(solution)/shard_map/ppermute | solution.py:17
  281.3 29.7 %collective-permute-start.7 = (bf16[256,1280]{0,1:T(8,128)(2,1)}, bf16[256,1280]{0,1:T(8,128)(2,1)}, u32[]{:S(2)}, u32[]{:S(2)}) collective-permute-start(bf16[256,1280]{0,1:T(8,128)(2,1)} %copy.18), channel_id=1, source_target_pairs={{0,1},{1,2},{2,3},{3,4},{4,5},{5,6},{6,7},{7,8},{8,9},{9,10},{10,1... | collective-permute-start | bytes 1966088 | tf_op jit(solution)/shard_map/ppermute | solution.py:17
  292.1 23.0 %copy-start.2 = (f32[5,256,2,128]{1,3,2,0:T(8,128)S(1)}, f32[5,256,2,128]{1,3,2,0:T(8,128)}, u32[]{:S(2)}) copy-start(f32[5,256,2,128]{1,3,2,0:T(8,128)} %custom-call.2) | copy-start | bytes 3932164
  313.3 1.8 copy-start.9
  315.1 34.4 %copy-start.5 = (bf16[256,1280]{1,0:T(8,128)(2,1)S(1)}, bf16[256,1280]{1,0:T(8,128)(2,1)}, u32[]{:S(2)}) copy-start(bf16[256,1280]{1,0:T(8,128)(2,1)} %param.9) | copy-start | bytes 1966084
Sparse Core Ops, SparseCore 0:
  11.4 66.9 all-gather.2
  98.0 172.6 reduce-scatter.1
  274.0 68.5 all-gather.4
where the time goes:
time: 367 us; the launch traced here: 366 us
  waiting for transfers between devices  242 us (66%)
  matrix products  48.8 us (13%)
  starting transfers between devices  23 us (6%)
  local copies, waits for them, and re-layouts  22 us (6%)
  between operations  14.1 us (4%)
  other arithmetic  12.6 us (3%)
    reduce_scatter x1, waiting for transfers between devices, per_device(): owner_sum = lax.psum_scatter(total, 'seq', scatter_dimension=0, tiled=True)  155 us
    all_gather x1, waiting for transfers between devices, per_device(): lax.all_gather(fast_weights.astype(jnp.bfloat16), 'seq', axis=1, tiled=True)  68.8 us
    ppermute x8, starting transfers between devices, from_behind(): return lax.ppermute(block, axis, route)  22.8 us
    ppermute x8, waiting for transfers between devices, from_behind(): return lax.ppermute(block, axis, route)  18.3 us
    dot_general x5, matrix products, one_group(): jnp.einsum('hqk,khd->qhd', att_probs, v_part, preferred_element_type=jnp....  13.9 us
    unnamed x32, local copies, waits for them, and re-layouts  12.9 us
    dot_general x8, matrix products, row_product(): lax.dot_general(left_side, right_side, (((1,), (1,)), ((), ())), preferre...  12.1 us
    sub x5, matrix products, one_group(): exp_scores = jnp.exp(scores - top_score)  11.6 us
  transfers between devices with their start and end apart: 11, of which 5 were waited for; matrix products, arithmetic and copies ran while one was open for 14% of the time, Pallas kernels for 0%

commit v1 on v0

v1 whole, which is shorter than its diff:
```python
import functools
import math

import jax
import jax.numpy as jnp
from jax import lax
from jax.experimental import pallas as pl
from jax.experimental.pallas import tpu as pltpu
from jax.sharding import PartitionSpec as P

ATT_DIM = 128
WINDOW = 1024


def silu_slope(values_in):
    sigmoid_val = jax.nn.sigmoid(values_in)
    return sigmoid_val * (1.0 + values_in * (1.0 - sigmoid_val))


def row_product(left_side, right_side):
    return lax.dot_general(
        left_side, right_side, (((1,), (1,)), ((), ())), preferred_element_type=jnp.float32
    )


def token_product(left_side, right_side):
    return lax.dot_general(
        left_side, right_side, (((0,), (0,)), ((), ())), preferred_element_type=jnp.float32
    )


def attention_kernel(tile, base_ref, q_ref, k_ref, v_ref, o_ref):
    tokens = q_ref.shape[0]
    span = tile + WINDOW
    base = base_ref[0]
    row = lax.broadcasted_iota(jnp.int32, (tile, span), 0)
    col = lax.broadcasted_iota(jnp.int32, (tile, span), 1)
    near = (col > row) & (col <= row + WINDOW)
    for lo in range(0, tokens, tile):
        scores = row_product(q_ref[lo : lo + tile, :], k_ref[lo : lo + span, :])
        scores = scores * (1.0 / math.sqrt(ATT_DIM))
        allowed = near & (col >= WINDOW - base - lo)
        scores = jnp.where(allowed, scores, -jnp.inf)
        exp_scores = jnp.exp(scores - jnp.max(scores, axis=-1, keepdims=True))
        total = jnp.sum(exp_scores, axis=-1, keepdims=True)
        attended = jnp.dot(
            exp_scores.astype(jnp.bfloat16),
            v_ref[lo : lo + span, :],
            preferred_element_type=jnp.float32,
        ) / total
        mean = jnp.mean(attended * attended, axis=-1, keepdims=True)
        o_ref[lo : lo + tile, :] = attended * lax.rsqrt(mean + 1e-06)


def window_attention(base, q, k, v):
    tokens, width = q.shape
    keys = k.shape[0]
    tile = min(256, tokens)
    heads = width // ATT_DIM
    work = heads * tokens * (tile + WINDOW)
    return pl.pallas_call(
        functools.partial(attention_kernel, tile),
        out_shape=jax.ShapeDtypeStruct((tokens, width), jnp.float32),
        grid=(heads,),
        in_specs=[
            pl.BlockSpec(memory_space=pltpu.SMEM),
            pl.BlockSpec((tokens, ATT_DIM), lambda a: (0, a)),
            pl.BlockSpec((keys, ATT_DIM), lambda a: (0, a)),
            pl.BlockSpec((keys, ATT_DIM), lambda a: (0, a)),
        ],
        out_specs=pl.BlockSpec((tokens, ATT_DIM), lambda a: (0, a)),
        compiler_params=pltpu.CompilerParams(vmem_limit_bytes=40 * 2**20),
        cost_estimate=pl.CostEstimate(
            flops=4 * work * ATT_DIM, bytes_accessed=4 * keys * width * 2, transcendentals=work
        ),
    )(base, q, k, v)


def per_device(queries, key_rows, value_rows, step_rates, fast_weights, momentum, out_gain):
    tokens = queries.shape[0]
    head_dim = fast_weights.shape[2]
    size = lax.axis_size("seq")
    me = lax.axis_index("seq")
    first_core = me % 2 == 0
    grad_scale = 1.0 / math.sqrt(tokens * size)
    pair = [(i, i ^ 1) for i in range(size)]
    half, quarter = size // 2, size // 4
    swap = []
    for i in range(size):
        head, m, core = i // half, (i % half) // 2, i % 2
        swap.append((i, core * half + m * 2 + head))
    same_core = [[i for i in range(size) if i % 2 == c] for c in range(2)]

    held16 = lax.ppermute(fast_weights.astype(jnp.bfloat16), "seq", swap)
    start_rows = lax.all_gather(
        held16, "seq", axis=1, tiled=True, axis_index_groups=same_core
    )

    rates = jnp.repeat(step_rates.T, head_dim, axis=1)
    out_grad = (-grad_scale * rates * value_rows.astype(jnp.float32)).astype(jnp.bfloat16)
    whole = jnp.stack([key_rows, value_rows, out_grad, queries])
    low, high = whole[:, :, :head_dim], whole[:, :, head_dim:]
    kept = jnp.where(first_core, low, high)
    came = lax.ppermute(jnp.where(first_core, high, low), "seq", pair)
    mine = jnp.concatenate(
        [jnp.where(first_core, kept, came), jnp.where(first_core, came, kept)], axis=1
    )
    keys, values, outs, asks = mine[0], mine[1], mine[2], mine[3]
    held_weights = lax.ppermute(fast_weights, "seq", swap)
    held_momentum = lax.ppermute(momentum, "seq", swap)

    reach = WINDOW // (2 * tokens)
    window = [mine[:2]]
    for hop in range(1, reach + 1):
        route = [(i, i + 2 * hop) for i in range(size - 2 * hop)]
        window.insert(0, lax.ppermute(mine[:2], "seq", route))
    window = jnp.concatenate(window, axis=1)

    key_gate = row_product(keys, start_rows[0])
    key_up = row_product(keys, start_rows[1])
    hidden_grad = row_product(outs, start_rows[2])
    key_hidden = (jax.nn.silu(key_gate) * key_up).astype(jnp.bfloat16)
    gate_grad = (hidden_grad * key_up * silu_slope(key_gate)).astype(jnp.bfloat16)
    up_grad = (hidden_grad * jax.nn.silu(key_gate)).astype(jnp.bfloat16)
    total = jnp.stack(
        [
            token_product(gate_grad, keys),
            token_product(up_grad, keys),
            token_product(key_hidden, outs),
        ],
        axis=1,
    ).astype(jnp.bfloat16)
    held_sum = lax.psum_scatter(
        total, "seq", scatter_dimension=0, tiled=True, axis_index_groups=same_core
    )
    window, total = lax.optimization_barrier((window, total))
    base = jnp.reshape((me // 2) * (2 * tokens), (1,)).astype(jnp.int32)
    att_normed = window_attention(base, asks, window[0], window[1])
    held_sum, att_normed = lax.optimization_barrier((held_sum, att_normed))

    gradient = jnp.transpose(held_sum.astype(jnp.float32), (1, 0, 2))
    new_momentum = 0.9 * held_momentum + gradient
    moved = held_weights - new_momentum
    keep_norm = jnp.sqrt(jnp.mean(held_weights * held_weights, axis=-1, keepdims=True))
    new_weights = (
        moved * keep_norm * lax.rsqrt(jnp.mean(moved * moved, axis=-1, keepdims=True) + 1e-06)
    )
    applied = lax.all_gather(
        new_weights.astype(jnp.bfloat16), "seq", axis=1, tiled=True, axis_index_groups=same_core
    )
    owned_weights = lax.ppermute(new_weights, "seq", swap)
    owned_momentum = lax.ppermute(new_momentum, "seq", swap)

    query_gate = row_product(asks, applied[0])
    query_up = row_product(asks, applied[1])
    query_hidden = (jax.nn.silu(query_gate) * query_up).astype(jnp.bfloat16)
    fast_out = jnp.dot(query_hidden, applied[2], preferred_element_type=jnp.float32)
    gain = jnp.where(first_core, out_gain[:head_dim], out_gain[head_dim:])
    fast_normed = (
        fast_out
        * lax.rsqrt(jnp.mean(fast_out * fast_out, axis=-1, keepdims=True) + 1e-06)
        * gain
    )
    layer = (fast_normed + att_normed).astype(jnp.bfloat16)
    early, late = layer[:tokens], layer[tokens:]
    stay = jnp.where(first_core, early, late)
    back = lax.ppermute(jnp.where(first_core, late, early), "seq", pair)
    layer_out = jnp.concatenate(
        [jnp.where(first_core, stay, back), jnp.where(first_core, back, stay)], axis=1
    )
    return (layer_out, owned_weights, owned_momentum)


def solution(mesh):
    placed = (
        P(("groups", "seq"), None),
        P(("groups", "seq"), None),
        P(("groups", "seq"), None),
        P(None, ("groups", "seq")),
        P(None, "seq", None),
        P("groups", "seq", None),
        P(),
    )
    return jax.shard_map(
        per_device,
        mesh=mesh,
        in_specs=placed,
        out_specs=(P(("groups", "seq"), None), P("groups", "seq", None), P("groups", "seq", None)),
        check_vma=False,
    )
```

time: 367 us -> 366 us (level)
  waiting for transfers between devices: 242 us -> 283 us
  matrix products: 48.8 us -> 12.4 us
  local copies, waits for them, and re-layouts: 22 us -> 8.84 us
  Pallas kernels: 0 us -> 8.41 us
  starting transfers between devices: 23 us -> 28 us
    reduce_scatter x1 -> x0, waiting for transfers between devices: 155 us -> none  [per_device(): owner_sum = lax.psum_scatter(total, 'seq', scatter_dimension=0, tiled=True)]
    unnamed x3 -> x4, waiting for transfers between devices: 0.05 us -> 123 us
    ppermute x8 -> x9, waiting for transfers between devices: 18.3 us -> 73.9 us  [the longest x2 55.2 us: per_device(): window.insert(0, lax.ppermute(mine[:2], 'seq', route))]
    all_gather x2, waiting for transfers between devices: 68.8 us -> 86.1 us  [the longest x1 63.3 us: per_device(): lax.all_gather(new_weights.astype(jnp.bfloat16), 'seq', axis=1, tiled=Tru...]
    dot_general x7 -> x1, matrix products: 18.7 us -> 3.24 us  [per_device(): jnp.dot(query_hidden, applied[2], preferred_element_type=jnp.float32)]
    sub x5 -> x0, matrix products: 11.6 us -> none  [one_group(): exp_scores = jnp.exp(scores - top_score)]
    pallas_call x0 -> x1, Pallas kernels: none -> 8.41 us  [window_attention(): pl.pallas_call(functools.partial(attention_kernel, tile), out_shape=jax.S...]
    unnamed x32 -> x30, local copies, waits for them, and re-layouts: 12.9 us -> 4.9 us
  transfers between devices with their start and end apart: 11 -> 12, of which waited for: 5 -> 8; matrix products, arithmetic and copies ran while one was open for 14% -> 3% of each run, Pallas kernels for 0% -> 2%
where the time goes in v1:
time: 366 us; the launch traced here: 365 us
  waiting for transfers between devices  283 us (77%)
  starting transfers between devices  28 us (8%)
  between operations  14.8 us (4%)
  matrix products  12.4 us (3%)
  other arithmetic  9.85 us (3%)
  local copies, waits for them, and re-layouts  8.84 us (2%)
  Pallas kernels  8.41 us (2%)
    unnamed x4, waiting for transfers between devices  123 us
    all_gather x1, waiting for transfers between devices, per_device(): lax.all_gather(new_weights.astype(jnp.bfloat16), 'seq', axis=1, tiled=Tru...  63.3 us
    ppermute x2, waiting for transfers between devices, per_device(): window.insert(0, lax.ppermute(mine[:2], 'seq', route))  55.2 us
    all_gather x1, waiting for transfers between devices, per_device(): lax.all_gather(held16, 'seq', axis=1, tiled=True, axis_index_groups=same_...  22.8 us
    ppermute x1, waiting for transfers between devices, per_device(): owned_weights = lax.ppermute(new_weights, 'seq', swap)  9.17 us
    pallas_call x1, Pallas kernels, window_attention(): pl.pallas_call(functools.partial(attention_kernel, tile), out_shape=jax.S...  8.41 us
  transfers between devices with their start and end apart: 12, of which 8 were waited for; matrix products, arithmetic and copies ran while one was open for 3% of the time, Pallas kernels for 2%

profile of v1, /device:TPU:1, one launch (start us, length us, event | category | flops | bytes accessed | tf_op | source)
XLA Modules:
  0.0 365.3 jit_solution(11487457334366019855)
XLA Ops:
  7.2 1.0 convert_element_type.31
  8.2 5.6 %collective-permute-start.3 = (bf16[3,40,640]{2,1,0:T(8,128)(2,1)S(1)}, bf16[3,40,640]{2,1,0:T(8,128)(2,1)S(1)}, u32[]{:S(2)}, u32[]{:S(2)}) collective-permute-start(bf16[3,40,640]{2,1,0:T(8,128)(2,1)S(1)} %convert_element_type.31), channel_id=1, source_target_pairs={{0,0},{1,16},{2,2},{3,18},{4,4},{5,20},{6,6},{7,22},{8,8},{9,24},{... | collective-permute-start | bytes 460808 | tf_op jit(solution)/shard_map/ppermute | solution.py:94
  15.2 3.2 collective-permute-done.3
  19.2 0.9 copy-done.5
  20.9 3.0 collective-permute-done
  24.4 3.2 collective-permute-start.4
  27.6 3.2 collective-permute-start.5
  30.8 0.9 fusion.14
  31.8 55.2 %collective-permute-done.4 = bf16[2,512,640]{2,1,0:T(8,128)(2,1)S(1)} collective-permute-done((bf16[2,512,640]{2,1,0:T(8,128)(2,1)S(1)}, bf16[2,512,640]{2,1,0:T(8,128)(2,1)S(1)}, u32[]{:S(2)}, u32[]{:S(2)}) %collective-permute-start.4) | collective-permute-done | bytes 1310752 | tf_op jit(solution)/shard_map/ppermute | solution.py:116
  87.0 2.0 pad_maximum_fusion
  89.1 22.8 %all-gather.3.cloned.1.call-done = bf16[3,640,640]{2,1,0:T(8,128)(2,1)} async-done(((bf16[3,40,640]{2,1,0:T(8,128)(2,1)}), bf16[3,640,640]{2,1,0:T(8,128)(2,1)}) %all-gather.3.cloned.1.call-update) | async-done | bytes 2457616 | tf_op jit(solution)/shard_map/all_gather | solution.py:95
  111.8 2.1 fusion.9
  115.5 0.8 fusion.8
  116.3 1.0 fusion.2
  118.1 1.8 pad_maximum_fusion.2
  120.0 0.9 copy-done.7
  120.9 6.0 %collective-permute-start.1 = (f32[3,40,640]{2,1,0:T(8,128)S(1)}, f32[3,40,640]{2,1,0:T(8,128)S(1)}, u32[]{:S(2)}, u32[]{:S(2)}) collective-permute-start(f32[3,40,640]{2,1,0:T(8,128)S(1)} %copy-done.7), channel_id=1, source_target_pairs={{0,0},{1,16},{2,2},{3,18},{4,4},{5,20},{6,6},{7,22},{8,8},{9,24},{... | collective-permute-start | bytes 921608 | tf_op jit(solution)/shard_map/ppermute | solution.py:109
  126.9 2.1 collective-permute-start.2
  130.3 2.5 slice_bitcast_fusion
  132.7 8.4 %shard_map.94 = f32[512,640]{1,0:T(8,128)S(1)} custom-call(s32[1]{0:T(128)} %bitcast.14.base_ref, bf16[512,640]{1,0:T(8,128)(2,1)S(1)} %get-tuple-element.18.q_ref, bf16[1536,640]{1,0:T(8,128)(2,1)S(1)} %get-tuple-element.15.k_ref, bf16[1536,640]{1,0:T(8,128)(2,1)S(1)} %get-tuple-element.14.v_ref), custom_call_target="tpu_custom_call" | custom-call | flops 1677721600 | bytes 7864320 | tf_op jit(solution)/shard_map/pallas_call | solution.py:61
  141.2 123.0 %all-reduce.3.cloned.1.call-done = bf16[640,3,640]{2,0,1:T(8,128)(2,1)} async-done(((bf16[640,3,640]{2,0,1:T(8,128)(2,1)}), bf16[640,3,640]{2,0,1:T(8,128)(2,1)}) %all-reduce.3.cloned.1.call-update) | async-done | bytes 2457616
  264.2 0.9 constant_dynamic-slice_fusion
  265.3 1.0 fusion.26
  266.3 63.3 %all-gather.5.cloned.1.call-done = bf16[3,640,640]{2,1,0:T(8,128)(2,1)} async-done(((bf16[3,40,640]{2,1,0:T(8,128)(2,1)}), bf16[3,640,640]{2,1,0:T(8,128)(2,1)}) %all-gather.5.cloned.1.call-update) | async-done | bytes 2457616 | tf_op jit(solution)/shard_map/all_gather | solution.py:148
  329.6 3.0 fusion.6
  332.6 3.2 multiply_reduce_fusion
  336.2 1.2 collective-permute-start.6
  337.4 4.2 %collective-permute-start.7 = (f32[3,40,640]{2,1,0:T(8,128)S(1)}, f32[3,40,640]{2,1,0:T(8,128)S(1)}, u32[]{:S(2)}, u32[]{:S(2)}) collective-permute-start(f32[3,40,640]{2,1,0:T(8,128)S(1)} %copy-done.8), channel_id=1, source_target_pairs={{0,0},{1,16},{2,2},{3,18},{4,4},{5,20},{6,6},{7,22},{8,8},{9,24},{... | collective-permute-start | bytes 921608 | tf_op jit(solution)/shard_map/ppermute | solution.py:151
  341.7 2.2 collective-permute-start.8
  343.9 9.2 %collective-permute-done.7 = f32[3,40,640]{2,1,0:T(8,128)S(1)} collective-permute-done((f32[3,40,640]{2,1,0:T(8,128)S(1)}, f32[3,40,640]{2,1,0:T(8,128)S(1)}, u32[]{:S(2)}, u32[]{:S(2)}) %collective-permute-start.7) | collective-permute-done | bytes 307232 | tf_op jit(solution)/shard_map/ppermute | solution.py:151
  353.1 3.3 collective-permute-done.8
  356.5 0.9 pad_maximum_fusion.4
  (57 shorter events, 8.4 us)
Async XLA Ops:
  7.2 104.7 %all-gather.3.cloned.1.call-start = ((), (), s32[]{:S(2)}) async-start(), calls=%async_computation | async-start | bytes 2611200 | tf_op jit(solution)/shard_map/all_gather | solution.py:95
  8.2 10.1 %collective-permute-start.3 = (bf16[3,40,640]{2,1,0:T(8,128)(2,1)S(1)}, bf16[3,40,640]{2,1,0:T(8,128)(2,1)S(1)}, u32[]{:S(2)}, u32[]{:S(2)}) collective-permute-start(bf16[3,40,640]{2,1,0:T(8,128)(2,1)S(1)} %convert_element_type.31), channel_id=1, source_target_pairs={{0,0},{1,16},{2,2},{3,18},{4,4},{5,20},{6,6},{7,22},{8,8},{9,24},{... | collective-permute-start | bytes 460808 | tf_op jit(solution)/shard_map/ppermute | solution.py:94
  15.1 4.0 %copy-start.1 = (bf16[256,1280]{1,0:T(8,128)(2,1)S(1)}, bf16[256,1280]{1,0:T(8,128)(2,1)}, u32[]{:S(2)}) copy-start(bf16[256,1280]{1,0:T(8,128)(2,1)} %param.9) | copy-start | bytes 1966084
  18.3 0.7 copy-start.9
  19.0 245.2 %all-reduce.3.cloned.1.call-start = ((), (), s32[]{:S(2)}) async-start(), calls=%async_computation.2 | async-start | bytes 4915200
  19.1 1.1 copy-start.5
  19.1 1.3 copy-start.6
  20.9 3.1 collective-permute-start
  24.4 62.6 %collective-permute-start.4 = (bf16[2,512,640]{2,1,0:T(8,128)(2,1)S(1)}, bf16[2,512,640]{2,1,0:T(8,128)(2,1)S(1)}, u32[]{:S(2)}, u32[]{:S(2)}) collective-permute-start(bf16[2,512,640]{2,1,0:T(8,128)(2,1)S(1)} %pad_maximum_fusion.3), channel_id=1, source_target_pairs={{0,4},{1,5},{2,6},{3,7},{4,8},{5,9},{6,10},{7,11},{8,12},{9,13},{1... | collective-permute-start | bytes 3932168 | tf_op jit(solution)/shard_map/ppermute | solution.py:116
  27.6 59.4 %collective-permute-start.5 = (bf16[2,512,640]{2,1,0:T(8,128)(2,1)S(1)}, bf16[2,512,640]{2,1,0:T(8,128)(2,1)S(1)}, u32[]{:S(2)}, u32[]{:S(2)}) collective-permute-start(bf16[2,512,640]{2,1,0:T(8,128)(2,1)S(1)} %pad_maximum_fusion.3), channel_id=1, source_target_pairs={{0,2},{1,3},{2,4},{3,5},{4,6},{5,7},{6,8},{7,9},{8,10},{9,11},{10,... | collective-permute-start | bytes 3932168 | tf_op jit(solution)/shard_map/ppermute | solution.py:116
  111.8 2.1 copy-start
  111.8 2.2 copy-start.2
  119.9 1.0 copy-start.7
  119.9 7.0 %copy-start.11 = (f32[3,40,640]{2,1,0:T(8,128)S(1)}, f32[3,40,640]{2,1,0:T(8,128)}, u32[]{:S(2)}) copy-start(f32[3,40,640]{2,1,0:T(8,128)} %param.12) | copy-start | bytes 921604
  119.9 9.1 %copy-start.12 = (u32[32]{0:T(128)S(1)}, u32[32]{0:T(128)}, u32[]{:S(2)}) copy-start(u32[32]{0:T(128)} %constant.56) | copy-start | bytes 388
  120.0 209.7 %all-gather.5.cloned.1.call-start = ((), (), s32[]{:S(2)}) async-start(), calls=%async_computation.1 | async-start | bytes 2611200 | tf_op jit(solution)/shard_map/all_gather | solution.py:148
  120.9 144.2 %collective-permute-start.1 = (f32[3,40,640]{2,1,0:T(8,128)S(1)}, f32[3,40,640]{2,1,0:T(8,128)S(1)}, u32[]{:S(2)}, u32[]{:S(2)}) collective-permute-start(f32[3,40,640]{2,1,0:T(8,128)S(1)} %copy-done.7), channel_id=1, source_target_pairs={{0,0},{1,16},{2,2},{3,18},{4,4},{5,20},{6,6},{7,22},{8,8},{9,24},{... | collective-permute-start | bytes 921608 | tf_op jit(solution)/shard_map/ppermute | solution.py:109
  126.9 138.2 %collective-permute-start.2 = (f32[3,40,640]{2,1,0:T(8,128)S(1)}, f32[3,40,640]{2,1,0:T(8,128)S(1)}, u32[]{:S(2)}, u32[]{:S(2)}) collective-permute-start(f32[3,40,640]{2,1,0:T(8,128)S(1)} %copy-done.11), channel_id=1, source_target_pairs={{0,0},{1,16},{2,2},{3,18},{4,4},{5,20},{6,6},{7,22},{8,8},{9,24},{... | collective-permute-start | bytes 921608 | tf_op jit(solution)/shard_map/ppermute | solution.py:110
  141.2 125.1 %copy-start.10 = (f32[1280]{0:T(1024)S(1)}, f32[1280]{0:T(1024)}, u32[]{:S(2)}) copy-start(f32[1280]{0:T(1024)} %param.13) | copy-start | bytes 15364
  265.3 1.0 copy-start.3
  335.9 1.6 copy-start.8
  335.9 5.8 %copy-start.4 = (f32[3,40,640]{2,1,0:T(8,128)S(1)}, f32[3,40,640]{2,1,0:T(8,128)}, u32[]{:S(2)}) copy-start(f32[3,40,640]{2,1,0:T(8,128)} %copy-done.3) | copy-start | bytes 921604
  336.2 20.2 %collective-permute-start.6 = (bf16[256,640]{1,0:T(8,128)(2,1)S(1)}, bf16[256,640]{1,0:T(8,128)(2,1)S(1)}, u32[]{:S(2)}, u32[]{:S(2)}) collective-permute-start(bf16[256,640]{1,0:T(8,128)(2,1)S(1)} %broadcast_select_fusion.6), channel_id=1, source_target_pairs={{0,1},{1,0},{2,3},{3,2},{4,5},{5,4},{6,7},{7,6},{8,9},{9,8},{10,11... | collective-permute-start | bytes 983048 | tf_op jit(solution)/shard_map/ppermute | solution.py:167
  337.4 15.6 %collective-permute-start.7 = (f32[3,40,640]{2,1,0:T(8,128)S(1)}, f32[3,40,640]{2,1,0:T(8,128)S(1)}, u32[]{:S(2)}, u32[]{:S(2)}) collective-permute-start(f32[3,40,640]{2,1,0:T(8,128)S(1)} %copy-done.8), channel_id=1, source_target_pairs={{0,0},{1,16},{2,2},{3,18},{4,4},{5,20},{6,6},{7,22},{8,8},{9,24},{... | collective-permute-start | bytes 921608 | tf_op jit(solution)/shard_map/ppermute | solution.py:151
  341.7 14.7 %collective-permute-start.8 = (f32[3,40,640]{2,1,0:T(8,128)S(1)}, f32[3,40,640]{2,1,0:T(8,128)S(1)}, u32[]{:S(2)}, u32[]{:S(2)}) collective-permute-start(f32[3,40,640]{2,1,0:T(8,128)S(1)} %copy-done.4), channel_id=1, source_target_pairs={{0,0},{1,16},{2,2},{3,18},{4,4},{5,20},{6,6},{7,22},{8,8},{9,24},{... | collective-permute-start | bytes 921608 | tf_op jit(solution)/shard_map/ppermute | solution.py:152
Sparse Core Ops, SparseCore 0:
  19.1 92.6 all-gather.2
  120.1 144.0 all-reduce.2
  267.5 62.0 all-gather.4

commit v2 on v1

--- a/solution.py
+++ b/solution.py
@@ -76,6 +76,200 @@
     )(base, q, k, v)
 
 
+MESH = pl.DeviceIdType.MESH
+
+
+def group_shape(size):
+    chips = size // 2
+    inner = 1
+    while inner * inner * 4 <= chips:
+        inner *= 2
+    return chips // inner, inner
+
+
+def place(outer, inner):
+    me = lax.axis_index("seq")
+    core = lax.rem(me, 2)
+    chip = lax.div(me, 2)
+    return lax.div(chip, inner), lax.rem(chip, inner), lambda i, j: {"seq": (i * inner + j) * 2 + core}
+
+
+def greet(outer, inner, a, b, device):
+    barrier = pltpu.get_barrier_semaphore()
+    for k in range(1, outer):
+        peer = device(lax.rem(a + k, outer), b)
+        pl.semaphore_signal(barrier, inc=1, device_id=peer, device_id_type=MESH)
+    for k in range(1, inner):
+        peer = device(a, lax.rem(b + k, inner))
+        pl.semaphore_signal(barrier, inc=1, device_id=peer, device_id_type=MESH)
+    pl.semaphore_wait(barrier, outer + inner - 2)
+
+
+def gather(outer, inner, a, b, device, shard, out, local_sem, send_sem, recv_sem):
+    def copy(src, slot, send, i, j):
+        return pltpu.make_async_remote_copy(
+            src_ref=src,
+            dst_ref=out.at[:, slot],
+            send_sem=send_sem.at[send],
+            recv_sem=recv_sem.at[slot],
+            device_id=device(i, j),
+            device_id_type=MESH,
+        )
+
+    own = a * inner + b
+    started = []
+
+    def start(src, slot, i, j):
+        one = copy(src, slot, len(started), i, j)
+        one.start()
+        started.append(one)
+
+    for k in range(1, outer):
+        start(shard, own, lax.rem(a + k, outer), b)
+    for k in range(1, inner):
+        start(shard, own, a, lax.rem(b + k, inner))
+    mine = pltpu.make_async_copy(shard, out.at[:, own], local_sem)
+    mine.start()
+    for k in range(1, outer):
+        slot = lax.rem(a + k, outer) * inner + b
+        copy(shard, slot, 0, lax.rem(a + 1, outer), b).wait_recv()
+        for n in range(1, inner):
+            start(out.at[:, slot], slot, a, lax.rem(b + n, inner))
+    for k in range(outer):
+        for n in range(1, inner):
+            slot = lax.rem(a + k, outer) * inner + lax.rem(b + n, inner)
+            copy(shard, slot, 0, lax.rem(a + 1, outer), b).wait_recv()
+    mine.wait()
+    for one in started:
+        one.wait_send()
+
+
+def gather_kernel(outer, inner, shard, out, local_sem, send_sem, recv_sem):
+    a, b, device = place(outer, inner)
+    greet(outer, inner, a, b, device)
+    gather(outer, inner, a, b, device, shard, out, local_sem, send_sem, recv_sem)
+
+
+def update_kernel(
+    outer, inner, part, weights, momentum, new_weights, new_momentum, out,
+    near, sums, far, own16, near_send, near_recv, far_send, far_recv,
+    local_sem, send_sem, recv_sem,
+):
+    a, b, device = place(outer, inner)
+    greet(outer, inner, a, b, device)
+    steps = list(range(1, outer)) + [0]
+    near_copies = {}
+    for j in steps:
+        for k in range(1, inner):
+            peer = lax.rem(b + k, inner)
+            one = pltpu.make_async_remote_copy(
+                src_ref=part.at[:, lax.rem(a + j, outer) * inner + peer],
+                dst_ref=near.at[k - 1, j],
+                send_sem=near_send.at[k - 1, j],
+                recv_sem=near_recv.at[k - 1, j],
+                device_id=device(a, peer),
+                device_id_type=MESH,
+            )
+            one.start()
+            near_copies[k, j] = one
+    far_copies = []
+    total = None
+    for j in steps:
+        target = lax.rem(a + j, outer)
+        total = part[:, target * inner + b].astype(jnp.float32)
+        for k in range(1, inner):
+            near_copies[k, j].wait_recv()
+            total = total + near[k - 1, j].astype(jnp.float32)
+        if j:
+            sums[j - 1] = total.astype(jnp.bfloat16)
+            one = pltpu.make_async_remote_copy(
+                src_ref=sums.at[j - 1],
+                dst_ref=far.at[j - 1],
+                send_sem=far_send.at[j - 1],
+                recv_sem=far_recv.at[j - 1],
+                device_id=device(target, b),
+                device_id_type=MESH,
+            )
+            one.start()
+            far_copies.append(one)
+    for j, one in enumerate(far_copies):
+        one.wait_recv()
+        total = total + far[j].astype(jnp.float32)
+    fast = weights[...]
+    moment = 0.9 * momentum[...] + total
+    new_momentum[...] = moment
+    moved = fast - moment
+    keep_norm = jnp.sqrt(jnp.mean(fast * fast, axis=-1, keepdims=True))
+    fresh = moved * keep_norm * lax.rsqrt(jnp.mean(moved * moved, axis=-1, keepdims=True) + 1e-06)
+    new_weights[...] = fresh
+    own16[...] = fresh.astype(jnp.bfloat16)
+    gather(outer, inner, a, b, device, own16, out, local_sem, send_sem, recv_sem)
+    for one in far_copies:
+        one.wait_send()
+    for one in near_copies.values():
+        one.wait_send()
+
+
+def gather_sems(outer, inner):
+    return [
+        pltpu.SemaphoreType.DMA,
+        pltpu.SemaphoreType.DMA((outer * inner - 1 + outer - 1 + inner,)),
+        pltpu.SemaphoreType.DMA((outer * inner,)),
+    ]
+
+
+def gathered(shard):
+    outer, inner = group_shape(lax.axis_size("seq"))
+    m, rows, width = shard.shape
+    vmem = pl.BlockSpec(memory_space=pltpu.VMEM)
+    out = pl.pallas_call(
+        functools.partial(gather_kernel, outer, inner),
+        out_shape=jax.ShapeDtypeStruct((m, outer * inner, rows, width), shard.dtype),
+        in_specs=[vmem],
+        out_specs=vmem,
+        scratch_shapes=gather_sems(outer, inner),
+        compiler_params=pltpu.CompilerParams(
+            collective_id=0, has_side_effects=True, vmem_limit_bytes=32 * 2**20
+        ),
+        cost_estimate=pl.CostEstimate(flops=0, bytes_accessed=10**8, transcendentals=0),
+    )(shard)
+    return out.reshape(m, outer * inner * rows, width)
+
+
+def updated(part, weights, momentum):
+    outer, inner = group_shape(lax.axis_size("seq"))
+    m, rows, width = weights.shape
+    vmem = pl.BlockSpec(memory_space=pltpu.VMEM)
+    block = (m, rows, width)
+    dma = pltpu.SemaphoreType.DMA
+    fresh, moment, out = pl.pallas_call(
+        functools.partial(update_kernel, outer, inner),
+        out_shape=(
+            jax.ShapeDtypeStruct(block, jnp.float32),
+            jax.ShapeDtypeStruct(block, jnp.float32),
+            jax.ShapeDtypeStruct((m, outer * inner, rows, width), jnp.bfloat16),
+        ),
+        in_specs=[vmem] * 3,
+        out_specs=(vmem,) * 3,
+        scratch_shapes=[
+            pltpu.VMEM((inner - 1, outer) + block, jnp.bfloat16),
+            pltpu.VMEM((outer - 1,) + block, jnp.bfloat16),
+            pltpu.VMEM((outer - 1,) + block, jnp.bfloat16),
+            pltpu.VMEM(block, jnp.bfloat16),
+            dma((inner - 1, outer)),
+            dma((inner - 1, outer)),
+            dma((outer - 1,)),
+            dma((outer - 1,)),
+        ]
+        + gather_sems(outer, inner),
+        compiler_params=pltpu.CompilerParams(
+            collective_id=1, has_side_effects=True, vmem_limit_bytes=40 * 2**20
+        ),
+        cost_estimate=pl.CostEstimate(flops=0, bytes_accessed=2 * 10**8, transcendentals=0),
+    )(part, weights, momentum)
+    return fresh, moment, out.reshape(m, outer * inner * rows, width)
+
+
 def per_device(queries, key_rows, value_rows, step_rates, fast_weights, momentum, out_gain):
     tokens = queries.shape[0]
     head_dim = fast_weights.shape[2]
@@ -89,12 +283,9 @@
     for i in range(size):
         head, m, core = i // half, (i % half) // 2, i % 2
         swap.append((i, core * half + m * 2 + head))
-    same_core = [[i for i in range(size) if i % 2 == c] for c in range(2)]
 
     held16 = lax.ppermute(fast_weights.astype(jnp.bfloat16), "seq", swap)
-    start_rows = lax.all_gather(
-        held16, "seq", axis=1, tiled=True, axis_index_groups=same_core
-    )
+    start_rows = gathered(held16)
 
     rates = jnp.repeat(step_rates.T, head_dim, axis=1)
     out_grad = (-grad_scale * rates * value_rows.astype(jnp.float32)).astype(jnp.bfloat16)
@@ -122,32 +313,18 @@
     key_hidden = (jax.nn.silu(key_gate) * key_up).astype(jnp.bfloat16)
     gate_grad = (hidden_grad * key_up * silu_slope(key_gate)).astype(jnp.bfloat16)
     up_grad = (hidden_grad * jax.nn.silu(key_gate)).astype(jnp.bfloat16)
+    rows = fast_weights.shape[1]
     total = jnp.stack(
         [
             token_product(gate_grad, keys),
             token_product(up_grad, keys),
             token_product(key_hidden, outs),
-        ],
-        axis=1,
-    ).astype(jnp.bfloat16)
-    held_sum = lax.psum_scatter(
-        total, "seq", scatter_dimension=0, tiled=True, axis_index_groups=same_core
-    )
-    window, total = lax.optimization_barrier((window, total))
+        ]
+    ).astype(jnp.bfloat16).reshape(3, half, rows, head_dim)
+    new_weights, new_momentum, applied = updated(total, held_weights, held_momentum)
+    window, applied = lax.optimization_barrier((window, applied))
     base = jnp.reshape((me // 2) * (2 * tokens), (1,)).astype(jnp.int32)
     att_normed = window_attention(base, asks, window[0], window[1])
-    held_sum, att_normed = lax.optimization_barrier((held_sum, att_normed))
-
-    gradient = jnp.transpose(held_sum.astype(jnp.float32), (1, 0, 2))
-    new_momentum = 0.9 * held_momentum + gradient
-    moved = held_weights - new_momentum
-    keep_norm = jnp.sqrt(jnp.mean(held_weights * held_weights, axis=-1, keepdims=True))
-    new_weights = (
-        moved * keep_norm * lax.rsqrt(jnp.mean(moved * moved, axis=-1, keepdims=True) + 1e-06)
-    )
-    applied = lax.all_gather(
-        new_weights.astype(jnp.bfloat16), "seq", axis=1, tiled=True, axis_index_groups=same_core
-    )
     owned_weights = lax.ppermute(new_weights, "seq", swap)
     owned_momentum = lax.ppermute(new_momentum, "seq", swap)
 

time: 366 us -> 244 us (0.67)
  the two profiles are of different devices: /device:TPU:1 before, /device:TPU:3 now
where the time goes in v2:
time: 244 us; the launch traced here: 243 us
  Pallas kernels  154 us (63%)
  starting transfers between devices  30 us (12%)
  waiting for transfers between devices  20.8 us (9%)
  local copies, waits for them, and re-layouts  14.9 us (6%)
  matrix products  12.3 us (5%)
  other arithmetic  10.5 us (4%)
    pallas_call x1, Pallas kernels, updated(): pl.pallas_call(functools.partial(update_kernel, outer, inner), out_shape=...  111 us
    pallas_call x1, Pallas kernels, gathered(): pl.pallas_call(functools.partial(gather_kernel, outer, inner), out_shape=...  34.4 us
    ppermute x1, waiting for transfers between devices, per_device(): owned_weights = lax.ppermute(new_weights, 'seq', swap)  9.18 us
    pallas_call x1, Pallas kernels, window_attention(): pl.pallas_call(functools.partial(attention_kernel, tile), out_shape=jax.S...  8.41 us
    ppermute x1, waiting for transfers between devices, per_device(): held16 = lax.ppermute(fast_weights.astype(jnp.bfloat16), 'seq', swap)  8.29 us
    ppermute x2, starting transfers between devices, per_device(): window.insert(0, lax.ppermute(mine[:2], 'seq', route))  7.88 us
    unnamed x29, local copies, waits for them, and re-layouts  7.08 us
    dot_general x4, matrix products, row_product(): lax.dot_general(left_side, right_side, (((1,), (1,)), ((), ())), preferre...  5.63 us
  transfers between devices with their start and end apart: 9, of which 3 were waited for; matrix products, arithmetic and copies ran while one was open for 6% of the time, Pallas kernels for 60%

profile of v2, /device:TPU:3, one launch (start us, length us, event | category | flops | bytes accessed | tf_op | source)
XLA Modules:
  0.0 243.3 jit_solution(11001144345062822019)
XLA Ops:
  2.0 1.0 copy-done.5
  3.1 0.9 copy-done.8
  4.8 1.3 copy-done.3
  6.8 4.1 %collective-permute-start.4 = (f32[3,40,640]{2,1,0:T(8,128)S(1)}, f32[3,40,640]{2,1,0:T(8,128)S(1)}, u32[]{:S(2)}, u32[]{:S(2)}) collective-permute-start(f32[3,40,640]{2,1,0:T(8,128)S(1)} %copy-done.11), channel_id=1, source_target_pairs={{0,0},{1,16},{2,2},{3,18},{4,4},{5,20},{6,6},{7,22},{8,8},{9,24},{... | collective-permute-start | bytes 921608 | tf_op jit(solution)/shard_map/ppermute | solution.py:300
  10.9 2.4 collective-permute-start.3
  13.3 4.1 %collective-permute-start.5 = (f32[3,40,640]{2,1,0:T(8,128)}, f32[3,40,640]{2,1,0:T(8,128)S(1)}, u32[]{:S(2)}, u32[]{:S(2)}) collective-permute-start(f32[3,40,640]{2,1,0:T(8,128)} %param.12), channel_id=1, source_target_pairs={{0,0},{1,16},{2,2},{3,18},{4,4},{5,20},{6,6},{7,22},{8,8},{9,24},{... | collective-permute-start | bytes 921608 | tf_op jit(solution)/shard_map/ppermute | solution.py:301
  17.4 8.3 %collective-permute-done.3.shard = bf16[3,40,640]{2,1,0:T(8,128)(2,1)S(1)} collective-permute-done((bf16[3,40,640]{2,1,0:T(8,128)(2,1)S(1)}, bf16[3,40,640]{2,1,0:T(8,128)(2,1)S(1)}, u32[]{:S(2)}, u32[]{:S(2)}) %collective-permute-start.3) | collective-permute-done | bytes 153632 | tf_op jit(solution)/shard_map/ppermute | solution.py:287
  25.7 34.4 %shard_map.94 = bf16[3,16,40,640]{3,2,1,0:T(8,128)(2,1)S(1)} custom-call(bf16[3,40,640]{2,1,0:T(8,128)(2,1)S(1)} %collective-permute-done.3.shard), custom_call_target="tpu_custom_call" | custom-call | bytes 100000000 | tf_op jit(solution)/shard_map/pallas_call | solution.py:225
  60.3 1.5 copy-done.4
  61.8 1.6 broadcast_select_fusion
  63.6 1.4 fusion.1
  65.0 2.9 %collective-permute-start.1 = (bf16[2,512,640]{2,1,0:T(8,128)(2,1)}, bf16[2,512,640]{2,1,0:T(8,128)(2,1)}, u32[]{:S(2)}, u32[]{:S(2)}) collective-permute-start(bf16[2,512,640]{2,1,0:T(8,128)(2,1)} %fusion.1), channel_id=1, source_target_pairs={{0,4},{1,5},{2,6},{3,7},{4,8},{5,9},{6,10},{7,11},{8,12},{9,13},{1... | collective-permute-start | bytes 3932168 | tf_op jit(solution)/shard_map/ppermute | solution.py:307
  68.0 4.9 %collective-permute-start.2 = (bf16[2,512,640]{2,1,0:T(8,128)(2,1)}, bf16[2,512,640]{2,1,0:T(8,128)(2,1)}, u32[]{:S(2)}, u32[]{:S(2)}) collective-permute-start(bf16[2,512,640]{2,1,0:T(8,128)(2,1)} %fusion.1), channel_id=1, source_target_pairs={{0,2},{1,3},{2,4},{3,5},{4,6},{5,7},{6,8},{7,9},{8,10},{9,11},{10,... | collective-permute-start | bytes 3932168 | tf_op jit(solution)/shard_map/ppermute | solution.py:307
  72.9 0.8 convolution_bitcast_fusion.1
  73.7 0.8 convolution_bitcast_fusion.2
  74.5 2.2 multiply_convert_fusion.2
  76.8 2.2 copy.15
  78.9 1.1 copy.16
  80.0 1.3 copy.17
  81.4 2.1 fusion.3
  85.8 110.9 %shard_map.95 = (f32[3,40,640]{2,1,0:T(8,128)S(1)}, f32[3,40,640]{2,1,0:T(8,128)S(1)}, bf16[3,16,40,640]{3,2,1,0:T(8,128)(2,1)S(1)}) custom-call(bf16[3,16,40,640]{3,2,1,0:T(8,128)(2,1)S(1)} %pad_maximum_fusion.2.part, f32[3,40,640]{2,1,0:T(8,128)S(1)} %collective-permute-done.4.weights, f32[3,40,640]{2,1,0:T(8,128)S(1)} %collective-permute-done.5.momentum), custom_call_target="tpu_custom_call" | custom-call | bytes 200000000 | tf_op jit(solution)/shard_map/pallas_call | solution.py:245
  196.8 4.4 %pad_maximum_fusion = bf16[2,1536,640]{2,1,0:T(8,128)(2,1)} fusion(bf16[2,512,640]{2,1,0:T(8,128)(2,1)} %fusion.1, bf16[2,512,640]{2,1,0:T(8,128)(2,1)} %collective-permute-done.2, bf16[2,512,640]{2,1,0:T(8,128)(2,1)} %collective-permute-done.1), kind=kLoop, calls=%fused_computation | loop fusion | flops 11796480 | bytes 7864320 | tf_op jit(solution)/shard_map/concatenate | solution.py:308
  201.2 1.9 fusion.10
  203.0 3.3 %multiply_reduce_fusion = (f32[512]{0:T(512)S(1)}, f32[512,640]{1,0:T(8,128)S(1)}) fusion(bf16[3,640,640]{2,1,0:T(8,128)(2,1)} %bitcast.76, bf16[512,640]{1,0:T(8,128)(2,1)S(1)} %get-tuple-element.21.q_ref, f32[512,640]{1,0:T(8,128)} %fusion.10), kind=kOutput, calls=%fused_computation.21 | convolution fusion | flops 841481728 | bytes 4917248 | tf_op jit(solution)/shard_map/dot_general | solution.py:334
  206.3 2.5 %slice_bitcast_fusion = (bf16[1536,640]{1,0:T(8,128)(2,1)S(1)}, bf16[1536,640]{1,0:T(8,128)(2,1)S(1)}) fusion(bf16[2,1536,640]{2,1,0:T(8,128)(2,1)} %pad_maximum_fusion), kind=kLoop, calls=%fused_computation.9 | loop fusion | bytes 7864320 | tf_op jit(solution)/shard_map/squeeze | solution.py:327
  208.8 8.4 %shard_map.96 = f32[512,640]{1,0:T(8,128)S(1)} custom-call(s32[1]{0:T(128)} %bitcast.26.base_ref, bf16[512,640]{1,0:T(8,128)(2,1)S(1)} %get-tuple-element.21.q_ref, bf16[1536,640]{1,0:T(8,128)(2,1)S(1)} %get-tuple-element.14.k_ref, bf16[1536,640]{1,0:T(8,128)(2,1)S(1)} %get-tuple-element.13.v_ref), custom_call_target="tpu_custom_call" | custom-call | flops 1677721600 | bytes 7864320 | tf_op jit(solution)/shard_map/pallas_call | solution.py:61
  217.5 4.5 %collective-permute-start.6 = (bf16[256,640]{1,0:T(8,128)(2,1)S(1)}, bf16[256,640]{1,0:T(8,128)(2,1)S(1)}, u32[]{:S(2)}, u32[]{:S(2)}) collective-permute-start(bf16[256,640]{1,0:T(8,128)(2,1)S(1)} %broadcast_select_fusion.6), channel_id=1, source_target_pairs={{0,1},{1,0},{2,3},{3,2},{4,5},{5,4},{6,7},{7,6},{8,9},{9,8},{10,11... | collective-permute-start | bytes 983048 | tf_op jit(solution)/shard_map/ppermute | solution.py:344
  222.0 1.9 collective-permute-start.7
  223.9 4.5 %collective-permute-start.8 = (f32[3,40,640]{2,1,0:T(8,128)S(1)}, f32[3,40,640]{2,1,0:T(8,128)S(1)}, u32[]{:S(2)}, u32[]{:S(2)}) collective-permute-start(f32[3,40,640]{2,1,0:T(8,128)S(1)} %get-tuple-element.12), channel_id=1, source_target_pairs={{0,0},{1,16},{2,2},{3,18},{4,4},{5,20},{6,6},{7,22},{8,8},{9,24},{... | collective-permute-start | bytes 921608 | tf_op jit(solution)/shard_map/ppermute | solution.py:329
  228.4 9.2 %collective-permute-done.7 = f32[3,40,640]{2,1,0:T(8,128)S(1)} collective-permute-done((f32[3,40,640]{2,1,0:T(8,128)S(1)}, f32[3,40,640]{2,1,0:T(8,128)S(1)}, u32[]{:S(2)}, u32[]{:S(2)}) %collective-permute-start.7) | collective-permute-done | bytes 307232 | tf_op jit(solution)/shard_map/ppermute | solution.py:328
  237.6 3.3 %collective-permute-done.8 = f32[3,40,640]{2,1,0:T(8,128)S(1)} collective-permute-done((f32[3,40,640]{2,1,0:T(8,128)S(1)}, f32[3,40,640]{2,1,0:T(8,128)S(1)}, u32[]{:S(2)}, u32[]{:S(2)}) %collective-permute-start.8) | collective-permute-done | bytes 307232 | tf_op jit(solution)/shard_map/ppermute | solution.py:329
  241.0 0.9 pad_maximum_fusion.4
  (49 shorter events, 7.3 us)
Async XLA Ops:
  1.9 1.1 copy-start.5
  3.0 1.1 copy-start.8
  3.0 1.3 copy-start.9
  4.6 1.5 copy-start.3
  4.6 2.2 copy-start.11
  4.6 12.8 %copy-start.12 = (f32[1280]{0:T(1024)S(1)}, f32[1280]{0:T(1024)}, u32[]{:S(2)}) copy-start(f32[1280]{0:T(1024)} %param.13) | copy-start | bytes 15364
  6.1 54.2 %collective-permute-start = (bf16[4,256,640]{2,1,0:T(8,128)(2,1)S(1)}, bf16[4,256,640]{2,1,0:T(8,128)(2,1)}, u32[]{:S(2)}, u32[]{:S(2)}) collective-permute-start(bf16[4,256,640]{2,1,0:T(8,128)(2,1)S(1)} %broadcast_select_fusion.2), channel_id=1, source_target_pairs={{0,1},{1,0},{2,3},{3,2},{4,5},{5,4},{6,7},{7,6},{8,9},{9,8},{10,11... | collective-permute-start | bytes 3932168 | tf_op jit(solution)/shard_map/ppermute | solution.py:295
  6.8 79.0 %collective-permute-start.4 = (f32[3,40,640]{2,1,0:T(8,128)S(1)}, f32[3,40,640]{2,1,0:T(8,128)S(1)}, u32[]{:S(2)}, u32[]{:S(2)}) collective-permute-start(f32[3,40,640]{2,1,0:T(8,128)S(1)} %copy-done.11), channel_id=1, source_target_pairs={{0,0},{1,16},{2,2},{3,18},{4,4},{5,20},{6,6},{7,22},{8,8},{9,24},{... | collective-permute-start | bytes 921608 | tf_op jit(solution)/shard_map/ppermute | solution.py:300
  10.9 14.8 %collective-permute-start.3 = (bf16[3,40,640]{2,1,0:T(8,128)(2,1)S(1)}, bf16[3,40,640]{2,1,0:T(8,128)(2,1)S(1)}, u32[]{:S(2)}, u32[]{:S(2)}) collective-permute-start(bf16[3,40,640]{2,1,0:T(8,128)(2,1)S(1)} %convert_element_type.31), channel_id=1, source_target_pairs={{0,0},{1,16},{2,2},{3,18},{4,4},{5,20},{6,6},{7,22},{8,8},{9,24},{... | collective-permute-start | bytes 460808 | tf_op jit(solution)/shard_map/ppermute | solution.py:287
  13.3 72.5 %collective-permute-start.5 = (f32[3,40,640]{2,1,0:T(8,128)}, f32[3,40,640]{2,1,0:T(8,128)S(1)}, u32[]{:S(2)}, u32[]{:S(2)}) collective-permute-start(f32[3,40,640]{2,1,0:T(8,128)} %param.12), channel_id=1, source_target_pairs={{0,0},{1,16},{2,2},{3,18},{4,4},{5,20},{6,6},{7,22},{8,8},{9,24},{... | collective-permute-start | bytes 921608 | tf_op jit(solution)/shard_map/ppermute | solution.py:301
  60.1 1.7 copy-start.4
  63.5 10.3 %copy-start.1 = (bf16[4,256,640]{2,1,0:T(8,128)(2,1)}, bf16[4,256,640]{2,1,0:T(8,128)(2,1)S(1)}, u32[]{:S(2)}) copy-start(bf16[4,256,640]{2,1,0:T(8,128)(2,1)S(1)} %get-tuple-element.16) | copy-start | bytes 3932164
  63.6 10.9 %copy-start.6 = (bf16[1,512,640]{2,1,0:T(8,128)(2,1)}, bf16[1,512,640]{2,1,0:T(8,128)(2,1)S(1)}, u32[]{:S(2)}) copy-start(bf16[1,512,640]{2,1,0:T(8,128)(2,1)S(1)} %get-tuple-element.20) | copy-start | bytes 1966084
  65.0 131.7 %collective-permute-start.1 = (bf16[2,512,640]{2,1,0:T(8,128)(2,1)}, bf16[2,512,640]{2,1,0:T(8,128)(2,1)}, u32[]{:S(2)}, u32[]{:S(2)}) collective-permute-start(bf16[2,512,640]{2,1,0:T(8,128)(2,1)} %fusion.1), channel_id=1, source_target_pairs={{0,4},{1,5},{2,6},{3,7},{4,8},{5,9},{6,10},{7,11},{8,12},{9,13},{1... | collective-permute-start | bytes 3932168 | tf_op jit(solution)/shard_map/ppermute | solution.py:307
  68.0 128.8 %collective-permute-start.2 = (bf16[2,512,640]{2,1,0:T(8,128)(2,1)}, bf16[2,512,640]{2,1,0:T(8,128)(2,1)}, u32[]{:S(2)}, u32[]{:S(2)}) collective-permute-start(bf16[2,512,640]{2,1,0:T(8,128)(2,1)} %fusion.1), channel_id=1, source_target_pairs={{0,2},{1,3},{2,4},{3,5},{4,6},{5,7},{6,8},{7,9},{8,10},{9,11},{10,... | collective-permute-start | bytes 3932168 | tf_op jit(solution)/shard_map/ppermute | solution.py:307
  81.4 2.1 copy-start.2
  83.5 1.1 copy-start.7
  83.5 1.3 copy-start.10
  196.7 4.4 %copy-start = (bf16[3,16,40,640]{3,2,1,0:T(8,128)(2,1)}, bf16[3,16,40,640]{3,2,1,0:T(8,128)(2,1)S(1)}, u32[]{:S(2)}) copy-start(bf16[3,16,40,640]{3,2,1,0:T(8,128)(2,1)S(1)} %get-tuple-element.8) | copy-start | bytes 7372804
  217.5 23.4 %collective-permute-start.6 = (bf16[256,640]{1,0:T(8,128)(2,1)S(1)}, bf16[256,640]{1,0:T(8,128)(2,1)S(1)}, u32[]{:S(2)}, u32[]{:S(2)}) collective-permute-start(bf16[256,640]{1,0:T(8,128)(2,1)S(1)} %broadcast_select_fusion.6), channel_id=1, source_target_pairs={{0,1},{1,0},{2,3},{3,2},{4,5},{5,4},{6,7},{7,6},{8,9},{9,8},{10,11... | collective-permute-start | bytes 983048 | tf_op jit(solution)/shard_map/ppermute | solution.py:344
  222.0 15.6 %collective-permute-start.7 = (f32[3,40,640]{2,1,0:T(8,128)S(1)}, f32[3,40,640]{2,1,0:T(8,128)S(1)}, u32[]{:S(2)}, u32[]{:S(2)}) collective-permute-start(f32[3,40,640]{2,1,0:T(8,128)S(1)} %get-tuple-element.11), channel_id=1, source_target_pairs={{0,0},{1,16},{2,2},{3,18},{4,4},{5,20},{6,6},{7,22},{8,8},{9,24},{... | collective-permute-start | bytes 921608 | tf_op jit(solution)/shard_map/ppermute | solution.py:328
  223.9 17.0 %collective-permute-start.8 = (f32[3,40,640]{2,1,0:T(8,128)S(1)}, f32[3,40,640]{2,1,0:T(8,128)S(1)}, u32[]{:S(2)}, u32[]{:S(2)}) collective-permute-start(f32[3,40,640]{2,1,0:T(8,128)S(1)} %get-tuple-element.12), channel_id=1, source_target_pairs={{0,0},{1,16},{2,2},{3,18},{4,4},{5,20},{6,6},{7,22},{8,8},{9,24},{... | collective-permute-start | bytes 921608 | tf_op jit(solution)/shard_map/ppermute | solution.py:329

commit v3 on v2

--- a/solution.py
+++ b/solution.py
@@ -29,7 +29,10 @@
     )
 
 
-def attention_kernel(tile, base_ref, q_ref, k_ref, v_ref, o_ref):
+def attention_kernel(tile, pieces, base_ref, q_ref, *refs):
+    o_ref = refs[pieces]
+    keys = jnp.concatenate([ref[0] for ref in refs[:pieces]], axis=0)
+    values = jnp.concatenate([ref[1] for ref in refs[:pieces]], axis=0)
     tokens = q_ref.shape[0]
     span = tile + WINDOW
     base = base_ref[0]
@@ -37,7 +40,7 @@
     col = lax.broadcasted_iota(jnp.int32, (tile, span), 1)
     near = (col > row) & (col <= row + WINDOW)
     for lo in range(0, tokens, tile):
-        scores = row_product(q_ref[lo : lo + tile, :], k_ref[lo : lo + span, :])
+        scores = row_product(q_ref[lo : lo + tile, :], keys[lo : lo + span])
         scores = scores * (1.0 / math.sqrt(ATT_DIM))
         allowed = near & (col >= WINDOW - base - lo)
         scores = jnp.where(allowed, scores, -jnp.inf)
@@ -45,46 +48,51 @@
         total = jnp.sum(exp_scores, axis=-1, keepdims=True)
         attended = jnp.dot(
             exp_scores.astype(jnp.bfloat16),
-            v_ref[lo : lo + span, :],
+            values[lo : lo + span],
             preferred_element_type=jnp.float32,
         ) / total
         mean = jnp.mean(attended * attended, axis=-1, keepdims=True)
         o_ref[lo : lo + tile, :] = attended * lax.rsqrt(mean + 1e-06)
 
 
-def window_attention(base, q, k, v):
+def window_attention(base, q, window):
     tokens, width = q.shape
-    keys = k.shape[0]
     tile = min(256, tokens)
     heads = width // ATT_DIM
     work = heads * tokens * (tile + WINDOW)
+    pair = pl.BlockSpec((2, tokens, ATT_DIM), lambda a: (0, 0, a))
     return pl.pallas_call(
-        functools.partial(attention_kernel, tile),
+        functools.partial(attention_kernel, tile, len(window)),
         out_shape=jax.ShapeDtypeStruct((tokens, width), jnp.float32),
         grid=(heads,),
         in_specs=[
             pl.BlockSpec(memory_space=pltpu.SMEM),
             pl.BlockSpec((tokens, ATT_DIM), lambda a: (0, a)),
-            pl.BlockSpec((keys, ATT_DIM), lambda a: (0, a)),
-            pl.BlockSpec((keys, ATT_DIM), lambda a: (0, a)),
-        ],
+        ]
+        + [pair] * len(window),
         out_specs=pl.BlockSpec((tokens, ATT_DIM), lambda a: (0, a)),
         compiler_params=pltpu.CompilerParams(vmem_limit_bytes=40 * 2**20),
         cost_estimate=pl.CostEstimate(
-            flops=4 * work * ATT_DIM, bytes_accessed=4 * keys * width * 2, transcendentals=work
+            flops=4 * work * ATT_DIM,
+            bytes_accessed=4 * len(window) * tokens * width,
+            transcendentals=work,
         ),
-    )(base, q, k, v)
+    )(base, q, *window)
 
 
 MESH = pl.DeviceIdType.MESH
 
 
+INNER = 4
+
+
 def group_shape(size):
-    chips = size // 2
-    inner = 1
-    while inner * inner * 4 <= chips:
-        inner *= 2
-    return chips // inner, inner
+    return size // 2 // INNER, INNER
+
+
+def sides(b):
+    x = b + 1 - 2 * lax.rem(b, 2)
+    return x, lax.rem(b + 2, INNER), lax.rem(x + 2, INNER)
 
 
 def place(outer, inner):
@@ -99,10 +107,9 @@
     for k in range(1, outer):
         peer = device(lax.rem(a + k, outer), b)
         pl.semaphore_signal(barrier, inc=1, device_id=peer, device_id_type=MESH)
-    for k in range(1, inner):
-        peer = device(a, lax.rem(b + k, inner))
-        pl.semaphore_signal(barrier, inc=1, device_id=peer, device_id_type=MESH)
-    pl.semaphore_wait(barrier, outer + inner - 2)
+    for peer in sides(b)[:2]:
+        pl.semaphore_signal(barrier, inc=1, device_id=device(a, peer), device_id_type=MESH)
+    pl.semaphore_wait(barrier, outer + 1)
 
 
 def gather(outer, inner, a, b, device, shard, out, local_sem, send_sem, recv_sem):
@@ -124,21 +131,38 @@
         one.start()
         started.append(one)
 
+    x, y, across = sides(b)
+
+    def slot_of(k, i):
+        return lax.rem(a + k, outer) * inner + i
+
+    def arrived(slot):
+        copy(shard, slot, 0, a, x).wait_recv()
+
+    def relay(k):
+        source, target = ((x, y), (y, x))[k % 2]
+        slot = slot_of(k, source)
+        arrived(slot)
+        start(out.at[:, slot], slot, a, target)
+
     for k in range(1, outer):
         start(shard, own, lax.rem(a + k, outer), b)
-    for k in range(1, inner):
-        start(shard, own, a, lax.rem(b + k, inner))
     mine = pltpu.make_async_copy(shard, out.at[:, own], local_sem)
     mine.start()
-    for k in range(1, outer):
-        slot = lax.rem(a + k, outer) * inner + b
-        copy(shard, slot, 0, lax.rem(a + 1, outer), b).wait_recv()
-        for n in range(1, inner):
-            start(out.at[:, slot], slot, a, lax.rem(b + n, inner))
     for k in range(outer):
-        for n in range(1, inner):
-            slot = lax.rem(a + k, outer) * inner + lax.rem(b + n, inner)
-            copy(shard, slot, 0, lax.rem(a + 1, outer), b).wait_recv()
+        slot = slot_of(k, b)
+        source = shard
+        if k:
+            arrived(slot)
+            source = out.at[:, slot]
+        start(source, slot, a, x)
+        start(source, slot, a, y)
+        if k:
+            relay(k - 1)
+    relay(outer - 1)
+    for k in range(outer):
+        arrived(slot_of(k, (y, x)[k % 2]))
+        arrived(slot_of(k, across))
     mine.wait()
     for one in started:
         one.wait_send()
@@ -152,34 +176,48 @@
 
 def update_kernel(
     outer, inner, part, weights, momentum, new_weights, new_momentum, out,
-    near, sums, far, own16, near_send, near_recv, far_send, far_recv,
+    near, mixed, sums, far, own16, near_send, near_recv, far_send, far_recv,
     local_sem, send_sem, recv_sem,
 ):
     a, b, device = place(outer, inner)
     greet(outer, inner, a, b, device)
     steps = list(range(1, outer)) + [0]
+    x, y, across = sides(b)
     near_copies = {}
+
+    def send_near(kind, j, src, peer):
+        one = pltpu.make_async_remote_copy(
+            src_ref=src,
+            dst_ref=near.at[kind, j],
+            send_sem=near_send.at[kind, j],
+            recv_sem=near_recv.at[kind, j],
+            device_id=device(a, peer),
+            device_id_type=MESH,
+        )
+        one.start()
+        near_copies[kind, j] = one
+
+    def block(j, i):
+        return lax.rem(a + j, outer) * inner + i
+
     for j in steps:
-        for k in range(1, inner):
-            peer = lax.rem(b + k, inner)
-            one = pltpu.make_async_remote_copy(
-                src_ref=part.at[:, lax.rem(a + j, outer) * inner + peer],
-                dst_ref=near.at[k - 1, j],
-                send_sem=near_send.at[k - 1, j],
-                recv_sem=near_recv.at[k - 1, j],
-                device_id=device(a, peer),
-                device_id_type=MESH,
-            )
-            one.start()
-            near_copies[k, j] = one
+        first = (x, y)[j % 2]
+        send_near(0, j, part.at[:, block(j, across)], first)
+        send_near(1, j, part.at[:, block(j, first)], first)
+    for j in steps:
+        second = (y, x)[j % 2]
+        near_copies[0, j].wait_recv()
+        both = part[:, block(j, second)].astype(jnp.float32) + near[0, j].astype(jnp.float32)
+        mixed[j] = both.astype(jnp.bfloat16)
+        send_near(2, j, mixed.at[j], second)
     far_copies = []
     total = None
     for j in steps:
         target = lax.rem(a + j, outer)
-        total = part[:, target * inner + b].astype(jnp.float32)
-        for k in range(1, inner):
-            near_copies[k, j].wait_recv()
-            total = total + near[k - 1, j].astype(jnp.float32)
+        total = part[:, block(j, b)].astype(jnp.float32)
+        for kind in (1, 2):
+            near_copies[kind, j].wait_recv()
+            total = total + near[kind, j].astype(jnp.float32)
         if j:
             sums[j - 1] = total.astype(jnp.bfloat16)
             one = pltpu.make_async_remote_copy(
@@ -213,7 +251,7 @@
 def gather_sems(outer, inner):
     return [
         pltpu.SemaphoreType.DMA,
-        pltpu.SemaphoreType.DMA((outer * inner - 1 + outer - 1 + inner,)),
+        pltpu.SemaphoreType.DMA((outer - 1 + 3 * outer,)),
         pltpu.SemaphoreType.DMA((outer * inner,)),
     ]
 
@@ -252,12 +290,13 @@
         in_specs=[vmem] * 3,
         out_specs=(vmem,) * 3,
         scratch_shapes=[
-            pltpu.VMEM((inner - 1, outer) + block, jnp.bfloat16),
+            pltpu.VMEM((3, outer) + block, jnp.bfloat16),
+            pltpu.VMEM((outer,) + block, jnp.bfloat16),
             pltpu.VMEM((outer - 1,) + block, jnp.bfloat16),
             pltpu.VMEM((outer - 1,) + block, jnp.bfloat16),
             pltpu.VMEM(block, jnp.bfloat16),
-            dma((inner - 1, outer)),
-            dma((inner - 1, outer)),
+            dma((3, outer)),
+            dma((3, outer)),
             dma((outer - 1,)),
             dma((outer - 1,)),
         ]
@@ -297,15 +336,22 @@
         [jnp.where(first_core, kept, came), jnp.where(first_core, came, kept)], axis=1
     )
     keys, values, outs, asks = mine[0], mine[1], mine[2], mine[3]
-    held_weights = lax.ppermute(fast_weights, "seq", swap)
-    held_momentum = lax.ppermute(momentum, "seq", swap)
+    held = lax.ppermute(jnp.stack([fast_weights, momentum]), "seq", swap)
 
     reach = WINDOW // (2 * tokens)
-    window = [mine[:2]]
-    for hop in range(1, reach + 1):
-        route = [(i, i + 2 * hop) for i in range(size - 2 * hop)]
-        window.insert(0, lax.ppermute(mine[:2], "seq", route))
-    window = jnp.concatenate(window, axis=1)
+    own_pair = mine[:2]
+    window = [own_pair]
+    if reach == 2:
+        ahead = [(i, i + 4) for i in range(size - 4)]
+        beside = [(i, i ^ 2) for i in range(size)]
+        distant = lax.ppermute(own_pair, "seq", ahead)
+        even_chip = (me // 2) % 2 == 0
+        close = lax.ppermute(jnp.where(even_chip, own_pair, distant), "seq", beside)
+        window = [distant, close, own_pair]
+    else:
+        for hop in range(1, reach + 1):
+            route = [(i, i + 2 * hop) for i in range(size - 2 * hop)]
+            window.insert(0, lax.ppermute(own_pair, "seq", route))
 
     key_gate = row_product(keys, start_rows[0])
     key_up = row_product(keys, start_rows[1])
@@ -321,12 +367,11 @@
             token_product(key_hidden, outs),
         ]
     ).astype(jnp.bfloat16).reshape(3, half, rows, head_dim)
-    new_weights, new_momentum, applied = updated(total, held_weights, held_momentum)
-    window, applied = lax.optimization_barrier((window, applied))
+    new_weights, new_momentum, applied = updated(total, held[0], held[1])
+    asks, applied = lax.optimization_barrier((asks, applied))
     base = jnp.reshape((me // 2) * (2 * tokens), (1,)).astype(jnp.int32)
-    att_normed = window_attention(base, asks, window[0], window[1])
-    owned_weights = lax.ppermute(new_weights, "seq", swap)
-    owned_momentum = lax.ppermute(new_momentum, "seq", swap)
+    att_normed = window_attention(base, asks, window)
+    owned = lax.ppermute(jnp.stack([new_weights, new_momentum]), "seq", swap)
 
     query_gate = row_product(asks, applied[0])
     query_up = row_product(asks, applied[1])
@@ -345,7 +390,7 @@
     layer_out = jnp.concatenate(
         [jnp.where(first_core, stay, back), jnp.where(first_core, back, stay)], axis=1
     )
-    return (layer_out, owned_weights, owned_momentum)
+    return (layer_out, owned[0], owned[1])
 
 
 def solution(mesh):

time: 244 us -> 209 us (0.86)
  the two profiles are of different devices: /device:TPU:3 before, /device:TPU:1 now
where the time goes in v3:
time: 209 us; the launch traced here: 207 us
  Pallas kernels  119 us (57%)
  waiting for transfers between devices  25.6 us (12%)
  starting transfers between devices  24.5 us (12%)
  matrix products  14.6 us (7%)
  local copies, waits for them, and re-layouts  13.1 us (6%)
  other arithmetic  9.59 us (5%)
    pallas_call x1, Pallas kernels, updated(): pl.pallas_call(functools.partial(update_kernel, outer, inner), out_shape=...  81.9 us
    pallas_call x1, Pallas kernels, gathered(): pl.pallas_call(functools.partial(gather_kernel, outer, inner), out_shape=...  28 us
    ppermute x1, waiting for transfers between devices, per_device(): held16 = lax.ppermute(fast_weights.astype(jnp.bfloat16), 'seq', swap)  15.1 us
    ppermute x1, starting transfers between devices, per_device(): owned = lax.ppermute(jnp.stack([new_weights, new_momentum]), 'seq', swap)  11.3 us
    ppermute x1, waiting for transfers between devices, per_device(): distant = lax.ppermute(own_pair, 'seq', ahead)  10.5 us
    pallas_call x1, Pallas kernels, window_attention(): pl.pallas_call(functools.partial(attention_kernel, tile, len(window)), ou...  9.09 us
    dot_general x4, matrix products, row_product(): lax.dot_general(left_side, right_side, (((1,), (1,)), ((), ())), preferre...  5.86 us
    ppermute x1, starting transfers between devices, per_device(): held = lax.ppermute(jnp.stack([fast_weights, momentum]), 'seq', swap)  5.54 us
  transfers between devices with their start and end apart: 7, of which 2 were waited for; matrix products, arithmetic and copies ran while one was open for 13% of the time, Pallas kernels for 57%

profile of v3, /device:TPU:1, one launch (start us, length us, event | category | flops | bytes accessed | tf_op | source)
XLA Modules:
  0.0 207.3 jit_solution(15326996946378691044)
XLA Ops:
  2.0 1.0 copy-done.6
  3.1 0.9 copy-done.12
  4.6 1.2 broadcast_select_fusion.3
  5.9 0.9 pad_maximum_fusion.4
  6.8 5.5 %collective-permute-start.2 = (f32[2,3,40,640]{3,2,1,0:T(8,128)}, f32[2,3,40,640]{3,2,1,0:T(8,128)S(1)}, u32[]{:S(2)}, u32[]{:S(2)}) collective-permute-start(f32[2,3,40,640]{3,2,1,0:T(8,128)} %pad_maximum_fusion.4), channel_id=1, source_target_pairs={{0,0},{1,16},{2,2},{3,18},{4,4},{5,20},{6,6},{7,22},{8,8},{9,24},{... | collective-permute-start | bytes 1843208 | tf_op jit(solution)/shard_map/ppermute | solution.py:339
  12.4 1.9 collective-permute-start.1
  14.3 0.8 slice_select_fusion
  15.1 15.1 %collective-permute-done.1.shard = bf16[3,40,640]{2,1,0:T(8,128)(2,1)S(1)} collective-permute-done((bf16[3,40,640]{2,1,0:T(8,128)(2,1)S(1)}, bf16[3,40,640]{2,1,0:T(8,128)(2,1)S(1)}, u32[]{:S(2)}, u32[]{:S(2)}) %collective-permute-start.1) | collective-permute-done | bytes 153632 | tf_op jit(solution)/shard_map/ppermute | solution.py:326
  30.2 28.0 %shard_map.94 = bf16[3,16,40,640]{3,2,1,0:T(8,128)(2,1)S(1)} custom-call(bf16[3,40,640]{2,1,0:T(8,128)(2,1)S(1)} %collective-permute-done.1.shard), custom_call_target="tpu_custom_call" | custom-call | bytes 100000000 | tf_op jit(solution)/shard_map/pallas_call | solution.py:263
  58.5 0.9 slice_bitcast_fusion.2
  59.3 1.6 broadcast_select_fusion.1
  61.1 0.8 convolution_bitcast_fusion.2
  61.9 2.5 %collective-permute-start.3 = (bf16[2,512,640]{2,1,0:T(8,128)(2,1)S(1)}, bf16[2,512,640]{2,1,0:T(8,128)(2,1)S(1)}, u32[]{:S(2)}, u32[]{:S(2)}) collective-permute-start(bf16[2,512,640]{2,1,0:T(8,128)(2,1)S(1)} %pad_maximum_fusion.2.refs_2_), channel_id=1, source_target_pairs={{0,4},{1,5},{2,6},{3,7},{4,8},{5,9},{6,10},{7,11},{8,12},{9,13},{1... | collective-permute-start | bytes 3932168 | tf_op jit(solution)/shard_map/ppermute | solution.py:347
  64.5 0.8 convolution_bitcast_fusion.1
  65.4 2.4 %multiply_convert_fusion.2 = (bf16[640,512]{0,1:T(8,128)(2,1)}, bf16[640,512]{0,1:T(8,128)(2,1)}, bf16[640,512]{0,1:T(8,128)(2,1)}) fusion(f32[640,512]{0,1:T(8,128)S(1)} %convolution_bitcast_fusion.2, f32[640,512]{0,1:T(8,128)S(1)} %convolution_bitcast_fusion.1, bf16[640,640]{1,0:T(8,128)(2,1)S(1)} %bitcast.94, bf16[1,512,640]{2,1,0:T(8,128)(2,1)S(1)} %get-tuple-element.18), kind=kOutput, calls=%fused_computation.21 | convolution fusion | flops 424345600 | bytes 6062080 | tf_op jit(solution)/shard_map/dot_general | solution.py:21
  67.8 2.2 %copy.17 = bf16[640,512]{1,0:T(8,128)(2,1)} copy(bf16[640,512]{0,1:T(8,128)(2,1)} %get-tuple-element.16) | data formatting | bytes 1310720 | tf_op jit(solution)/shard_map/convert_element_type | solution.py:359
  69.9 2.2 %copy.16 = bf16[640,512]{1,0:T(8,128)(2,1)} copy(bf16[640,512]{0,1:T(8,128)(2,1)} %get-tuple-element.17) | data formatting | bytes 1310720 | tf_op jit(solution)/shard_map/convert_element_type | solution.py:361
  72.1 2.2 %copy.15 = bf16[640,512]{1,0:T(8,128)(2,1)} copy(bf16[640,512]{0,1:T(8,128)(2,1)} %get-tuple-element.15) | data formatting | bytes 1310720 | tf_op jit(solution)/shard_map/convert_element_type | solution.py:360
  74.3 2.1 %fusion.3 = bf16[1,16,40,640]{3,2,1,0:T(8,128)(2,1)S(1)} fusion(bf16[16,40,512]{2,1,0:T(8,128)(2,1)} %bitcast.98, bf16[1,512,640]{2,1,0:T(8,128)(2,1)} %copy-done.8), kind=kOutput, calls=%fused_computation.31 | convolution fusion | flops 419840000 | bytes 2129920 | tf_op jit(solution)/shard_map/dot_general | solution.py:27
  76.4 1.7 fusion.4
  78.1 10.5 %collective-permute-done.3.refs_0_ = bf16[2,512,640]{2,1,0:T(8,128)(2,1)S(1)} collective-permute-done((bf16[2,512,640]{2,1,0:T(8,128)(2,1)S(1)}, bf16[2,512,640]{2,1,0:T(8,128)(2,1)S(1)}, u32[]{:S(2)}, u32[]{:S(2)}) %collective-permute-start.3) | collective-permute-done | bytes 1310752 | tf_op jit(solution)/shard_map/ppermute | solution.py:347
  88.6 1.2 broadcast_select_fusion
  89.8 0.8 collective-permute-start.4
  92.3 81.9 %shard_map.95 = (f32[3,40,640]{2,1,0:T(8,128)S(1)}, f32[3,40,640]{2,1,0:T(8,128)S(1)}, bf16[3,16,40,640]{3,2,1,0:T(8,128)(2,1)S(1)}) custom-call(bf16[3,16,40,640]{3,2,1,0:T(8,128)(2,1)S(1)} %pad_maximum_fusion.1.part, f32[3,40,640]{2,1,0:T(8,128)S(1)} %copy-done.1, f32[3,40,640]{2,1,0:T(8,128)S(1)} %copy-done), custom_call_target="tpu_custom_call" | custom-call | bytes 200000000 | tf_op jit(solution)/shard_map/pallas_call | solution.py:283
  174.2 0.9 pad_maximum_fusion.5
  175.1 11.3 %collective-permute-start.6 = (f32[2,3,40,640]{3,2,1,0:T(8,128)}, f32[2,3,40,640]{3,2,1,0:T(8,128)}, u32[]{:S(2)}, u32[]{:S(2)}) collective-permute-start(f32[2,3,40,640]{3,2,1,0:T(8,128)} %pad_maximum_fusion.5), channel_id=1, source_target_pairs={{0,0},{1,16},{2,2},{3,18},{4,4},{5,20},{6,6},{7,22},{8,8},{9,24},{... | collective-permute-start | bytes 1843208 | tf_op jit(solution)/shard_map/ppermute | solution.py:374
  186.5 1.9 fusion.9
  188.3 4.3 %multiply_reduce_fusion = (f32[512]{0:T(512)S(1)}, f32[512,640]{1,0:T(8,128)}) fusion(bf16[3,640,640]{2,1,0:T(8,128)(2,1)} %bitcast.86, bf16[512,640]{1,0:T(8,128)(2,1)S(1)} %get-tuple-element.9.q_ref, f32[512,640]{1,0:T(8,128)} %fusion.9), kind=kOutput, calls=%fused_computation.18 | convolution fusion | flops 841481728 | bytes 4917248 | tf_op jit(solution)/shard_map/dot_general | solution.py:379
  192.6 9.1 %shard_map.96 = f32[512,640]{1,0:T(8,128)S(1)} custom-call(s32[1]{0:T(128)} %bitcast.30.base_ref, bf16[512,640]{1,0:T(8,128)(2,1)S(1)} %get-tuple-element.9.q_ref, bf16[2,512,640]{2,1,0:T(8,128)(2,1)S(1)} %collective-permute-done.3.refs_0_, bf16[2,512,640]{2,1,0:T(8,128)(2,1)} %collective-permute-done.4.refs_1_, ...), custom_call_target="tpu_custom_call" | custom-call | flops 1677721600 | bytes 3932160 | tf_op jit(solution)/shard_map/pallas_call | solution.py:64
  202.0 2.5 %collective-permute-start.5 = (bf16[256,640]{1,0:T(8,128)(2,1)S(1)}, bf16[256,640]{1,0:T(8,128)(2,1)S(1)}, u32[]{:S(2)}, u32[]{:S(2)}) collective-permute-start(bf16[256,640]{1,0:T(8,128)(2,1)S(1)} %broadcast_select_fusion.7), channel_id=1, source_target_pairs={{0,1},{1,0},{2,3},{3,2},{4,5},{5,4},{6,7},{7,6},{8,9},{9,8},{10,11... | collective-permute-start | bytes 983048 | tf_op jit(solution)/shard_map/ppermute | solution.py:389
  204.4 1.9 slice_bitcast_fusion
  206.4 0.9 pad_maximum_fusion.3
  (52 shorter events, 4.7 us)
Async XLA Ops:
  1.9 1.1 copy-start.6
  3.0 1.1 copy-start.12
  3.0 1.3 copy-start.13
  4.6 1.3 copy-start.11
  4.6 1.3 copy-start.15
  5.8 53.5 %collective-permute-start = (bf16[4,256,640]{2,1,0:T(8,128)(2,1)}, bf16[4,256,640]{2,1,0:T(8,128)(2,1)}, u32[]{:S(2)}, u32[]{:S(2)}) collective-permute-start(bf16[4,256,640]{2,1,0:T(8,128)(2,1)} %broadcast_select_fusion.3), channel_id=1, source_target_pairs={{0,1},{1,0},{2,3},{3,2},{4,5},{5,4},{6,7},{7,6},{8,9},{9,8},{10,11... | collective-permute-start | bytes 3932168 | tf_op jit(solution)/shard_map/ppermute | solution.py:334
  6.8 51.7 %collective-permute-start.2 = (f32[2,3,40,640]{3,2,1,0:T(8,128)}, f32[2,3,40,640]{3,2,1,0:T(8,128)S(1)}, u32[]{:S(2)}, u32[]{:S(2)}) collective-permute-start(f32[2,3,40,640]{3,2,1,0:T(8,128)} %pad_maximum_fusion.4), channel_id=1, source_target_pairs={{0,0},{1,16},{2,2},{3,18},{4,4},{5,20},{6,6},{7,22},{8,8},{9,24},{... | collective-permute-start | bytes 1843208 | tf_op jit(solution)/shard_map/ppermute | solution.py:339
  12.4 17.9 %collective-permute-start.1 = (bf16[3,40,640]{2,1,0:T(8,128)(2,1)S(1)}, bf16[3,40,640]{2,1,0:T(8,128)(2,1)S(1)}, u32[]{:S(2)}, u32[]{:S(2)}) collective-permute-start(bf16[3,40,640]{2,1,0:T(8,128)(2,1)S(1)} %convert_element_type.31), channel_id=1, source_target_pairs={{0,0},{1,16},{2,2},{3,18},{4,4},{5,20},{6,6},{7,22},{8,8},{9,24},{... | collective-permute-start | bytes 460808 | tf_op jit(solution)/shard_map/ppermute | solution.py:326
  61.0 3.4 %copy-start.3 = (bf16[4,256,640]{2,1,0:T(8,128)(2,1)}, bf16[4,256,640]{2,1,0:T(8,128)(2,1)S(1)}, u32[]{:S(2)}) copy-start(bf16[4,256,640]{2,1,0:T(8,128)(2,1)S(1)} %get-tuple-element.13) | copy-start | bytes 3932164
  61.0 3.4 %copy-start.5 = (bf16[4,256,640]{2,1,0:T(8,128)(2,1)}, bf16[4,256,640]{2,1,0:T(8,128)(2,1)S(1)}, u32[]{:S(2)}) copy-start(bf16[4,256,640]{2,1,0:T(8,128)(2,1)S(1)} %get-tuple-element.14) | copy-start | bytes 3932164
  61.9 26.7 %collective-permute-start.3 = (bf16[2,512,640]{2,1,0:T(8,128)(2,1)S(1)}, bf16[2,512,640]{2,1,0:T(8,128)(2,1)S(1)}, u32[]{:S(2)}, u32[]{:S(2)}) collective-permute-start(bf16[2,512,640]{2,1,0:T(8,128)(2,1)S(1)} %pad_maximum_fusion.2.refs_2_), channel_id=1, source_target_pairs={{0,4},{1,5},{2,6},{3,7},{4,8},{5,9},{6,10},{7,11},{8,12},{9,13},{1... | collective-permute-start | bytes 3932168 | tf_op jit(solution)/shard_map/ppermute | solution.py:347
  64.5 0.9 copy-start.8
  74.3 2.1 %copy-start.4 = (bf16[4,256,640]{2,1,0:T(8,128)(2,1)S(1)}, bf16[4,256,640]{2,1,0:T(8,128)(2,1)}, u32[]{:S(2)}) copy-start(bf16[4,256,640]{2,1,0:T(8,128)(2,1)} %copy-done.3) | copy-start | bytes 3932164
  74.3 2.1 %copy-start.7 = (bf16[640,512]{1,0:T(8,128)(2,1)S(1)}, bf16[640,512]{1,0:T(8,128)(2,1)}, u32[]{:S(2)}) copy-start(bf16[640,512]{1,0:T(8,128)(2,1)} %copy.17) | copy-start | bytes 1966084
  78.1 12.5 %copy-start.9 = (bf16[1,512,640]{2,1,0:T(8,128)(2,1)S(1)}, bf16[1,512,640]{2,1,0:T(8,128)(2,1)}, u32[]{:S(2)}) copy-start(bf16[1,512,640]{2,1,0:T(8,128)(2,1)} %copy-done.8) | copy-start | bytes 1966084
  78.1 12.4 %copy-start.14 = (bf16[640,512]{1,0:T(8,128)(2,1)S(1)}, bf16[640,512]{1,0:T(8,128)(2,1)}, u32[]{:S(2)}) copy-start(bf16[640,512]{1,0:T(8,128)(2,1)} %copy.15) | copy-start | bytes 1966084
  89.8 102.8 %collective-permute-start.4 = (bf16[2,512,640]{2,1,0:T(8,128)(2,1)}, bf16[2,512,640]{2,1,0:T(8,128)(2,1)}, u32[]{:S(2)}, u32[]{:S(2)}) collective-permute-start(bf16[2,512,640]{2,1,0:T(8,128)(2,1)} %broadcast_select_fusion), channel_id=1, source_target_pairs={{0,2},{1,3},{2,0},{3,1},{4,6},{5,7},{6,4},{7,5},{8,10},{9,11},{10,... | collective-permute-start | bytes 3932168 | tf_op jit(solution)/shard_map/ppermute | solution.py:349
  91.2 1.0 copy-start
  91.2 1.1 copy-start.1
  174.2 12.3 %copy-start.2 = (bf16[3,16,40,640]{3,2,1,0:T(8,128)(2,1)}, bf16[3,16,40,640]{3,2,1,0:T(8,128)(2,1)S(1)}, u32[]{:S(2)}) copy-start(bf16[3,16,40,640]{3,2,1,0:T(8,128)(2,1)S(1)} %get-tuple-element.8) | copy-start | bytes 7372804
  175.1 29.3 %collective-permute-start.6 = (f32[2,3,40,640]{3,2,1,0:T(8,128)}, f32[2,3,40,640]{3,2,1,0:T(8,128)}, u32[]{:S(2)}, u32[]{:S(2)}) collective-permute-start(f32[2,3,40,640]{3,2,1,0:T(8,128)} %pad_maximum_fusion.5), channel_id=1, source_target_pairs={{0,0},{1,16},{2,2},{3,18},{4,4},{5,20},{6,6},{7,22},{8,8},{9,24},{... | collective-permute-start | bytes 1843208 | tf_op jit(solution)/shard_map/ppermute | solution.py:374
  192.6 9.1 %copy-start.10 = (f32[512,640]{1,0:T(8,128)S(1)}, f32[512,640]{1,0:T(8,128)}, u32[]{:S(2)}) copy-start(f32[512,640]{1,0:T(8,128)} %get-tuple-element.30) | copy-start | bytes 3932164
  202.0 4.4 %collective-permute-start.5 = (bf16[256,640]{1,0:T(8,128)(2,1)S(1)}, bf16[256,640]{1,0:T(8,128)(2,1)S(1)}, u32[]{:S(2)}, u32[]{:S(2)}) collective-permute-start(bf16[256,640]{1,0:T(8,128)(2,1)S(1)} %broadcast_select_fusion.7), channel_id=1, source_target_pairs={{0,1},{1,0},{2,3},{3,2},{4,5},{5,4},{6,7},{7,6},{8,9},{9,8},{10,11... | collective-permute-start | bytes 983048 | tf_op jit(solution)/shard_map/ppermute | solution.py:389

commit v4 on v3

--- a/solution.py
+++ b/solution.py
@@ -102,14 +102,62 @@
     return lax.div(chip, inner), lax.rem(chip, inner), lambda i, j: {"seq": (i * inner + j) * 2 + core}
 
 
+def swap_partner(outer, inner):
+    me = lax.axis_index("seq")
+    half = outer * inner
+    head, core = lax.div(me, half), lax.rem(me, 2)
+    m = lax.div(lax.rem(me, half), 2)
+    return head != core, head == core, {"seq": core * half + m * 2 + head}
+
+
+def trade(outer, inner, moves):
+    goes, stays, partner = swap_partner(outer, inner)
+
+    def each(do_remote, do_local):
+        @pl.when(goes)
+        def _():
+            for src, dst, send, recv in moves:
+                do_remote(
+                    pltpu.make_async_remote_copy(
+                        src_ref=src,
+                        dst_ref=dst,
+                        send_sem=send,
+                        recv_sem=recv,
+                        device_id=partner,
+                        device_id_type=MESH,
+                    )
+                )
+
+        @pl.when(stays)
+        def _():
+            for src, dst, send, recv in moves:
+                do_local(pltpu.make_async_copy(src, dst, recv))
+
+    each(lambda one: one.start(), lambda one: one.start())
+    return lambda: each(lambda one: one.wait(), lambda one: one.wait())
+
+
 def greet(outer, inner, a, b, device):
     barrier = pltpu.get_barrier_semaphore()
+    goes, stays, partner = swap_partner(outer, inner)
+
+    @pl.when(goes)
+    def _():
+        pl.semaphore_signal(barrier, inc=1, device_id=partner, device_id_type=MESH)
+
     for k in range(1, outer):
         peer = device(lax.rem(a + k, outer), b)
         pl.semaphore_signal(barrier, inc=1, device_id=peer, device_id_type=MESH)
     for peer in sides(b)[:2]:
         pl.semaphore_signal(barrier, inc=1, device_id=device(a, peer), device_id_type=MESH)
-    pl.semaphore_wait(barrier, outer + 1)
+
+    @pl.when(goes)
+    def _():
+        pl.semaphore_wait(barrier, outer + 2)
+
+    @pl.when(stays)
+    def _():
+        pl.semaphore_wait(barrier, outer + 1)
 
 
 def gather(outer, inner, a, b, device, shard, out, local_sem, send_sem, recv_sem):
@@ -168,19 +216,29 @@
         one.wait_send()
 
 
-def gather_kernel(outer, inner, shard, out, local_sem, send_sem, recv_sem):
+def gather_kernel(outer, inner, own, out, shard, trade_sem, local_sem, send_sem, recv_sem):
     a, b, device = place(outer, inner)
     greet(outer, inner, a, b, device)
+    trade(outer, inner, [(own, shard, trade_sem.at[0], trade_sem.at[1])])()
     gather(outer, inner, a, b, device, shard, out, local_sem, send_sem, recv_sem)
 
 
 def update_kernel(
-    outer, inner, part, weights, momentum, new_weights, new_momentum, out,
+    outer, inner, part, own_weights, own_momentum, new_weights, new_momentum, out,
+    weights, momentum, fresh_weights, fresh_momentum, trade_sem,
     near, mixed, sums, far, own16, near_send, near_recv, far_send, far_recv,
     local_sem, send_sem, recv_sem,
 ):
     a, b, device = place(outer, inner)
     greet(outer, inner, a, b, device)
+    take = trade(
+        outer,
+        inner,
+        [
+            (own_weights, weights, trade_sem.at[0], trade_sem.at[1]),
+            (own_momentum, momentum, trade_sem.at[2], trade_sem.at[3]),
+        ],
+    )
     steps = list(range(1, outer)) + [0]
     x, y, across = sides(b)
     near_copies = {}
@@ -233,15 +291,25 @@
     for j, one in enumerate(far_copies):
         one.wait_recv()
         total = total + far[j].astype(jnp.float32)
+    take()
     fast = weights[...]
     moment = 0.9 * momentum[...] + total
-    new_momentum[...] = moment
+    fresh_momentum[...] = moment
     moved = fast - moment
     keep_norm = jnp.sqrt(jnp.mean(fast * fast, axis=-1, keepdims=True))
     fresh = moved * keep_norm * lax.rsqrt(jnp.mean(moved * moved, axis=-1, keepdims=True) + 1e-06)
-    new_weights[...] = fresh
+    fresh_weights[...] = fresh
     own16[...] = fresh.astype(jnp.bfloat16)
+    give = trade(
+        outer,
+        inner,
+        [
+            (fresh_weights, new_weights, trade_sem.at[4], trade_sem.at[5]),
+            (fresh_momentum, new_momentum, trade_sem.at[6], trade_sem.at[7]),
+        ],
+    )
     gather(outer, inner, a, b, device, own16, out, local_sem, send_sem, recv_sem)
+    give()
     for one in far_copies:
         one.wait_send()
     for one in near_copies.values():
@@ -265,7 +333,8 @@
         out_shape=jax.ShapeDtypeStruct((m, outer * inner, rows, width), shard.dtype),
         in_specs=[vmem],
         out_specs=vmem,
-        scratch_shapes=gather_sems(outer, inner),
+        scratch_shapes=[pltpu.VMEM(shard.shape, shard.dtype), pltpu.SemaphoreType.DMA((2,))]
+        + gather_sems(outer, inner),
         compiler_params=pltpu.CompilerParams(
             collective_id=0, has_side_effects=True, vmem_limit_bytes=32 * 2**20
         ),
@@ -290,6 +359,11 @@
         in_specs=[vmem] * 3,
         out_specs=(vmem,) * 3,
         scratch_shapes=[
+            pltpu.VMEM(block, jnp.float32),
+            pltpu.VMEM(block, jnp.float32),
+            pltpu.VMEM(block, jnp.float32),
+            pltpu.VMEM(block, jnp.float32),
+            dma((8,)),
             pltpu.VMEM((3, outer) + block, jnp.bfloat16),
             pltpu.VMEM((outer,) + block, jnp.bfloat16),
             pltpu.VMEM((outer - 1,) + block, jnp.bfloat16),
@@ -317,14 +391,8 @@
     first_core = me % 2 == 0
     grad_scale = 1.0 / math.sqrt(tokens * size)
     pair = [(i, i ^ 1) for i in range(size)]
-    half, quarter = size // 2, size // 4
-    swap = []
-    for i in range(size):
-        head, m, core = i // half, (i % half) // 2, i % 2
-        swap.append((i, core * half + m * 2 + head))
-
-    held16 = lax.ppermute(fast_weights.astype(jnp.bfloat16), "seq", swap)
-    start_rows = gathered(held16)
+    half = size // 2
+    start_rows = gathered(fast_weights.astype(jnp.bfloat16))
 
     rates = jnp.repeat(step_rates.T, head_dim, axis=1)
     out_grad = (-grad_scale * rates * value_rows.astype(jnp.float32)).astype(jnp.bfloat16)
@@ -336,7 +404,6 @@
         [jnp.where(first_core, kept, came), jnp.where(first_core, came, kept)], axis=1
     )
     keys, values, outs, asks = mine[0], mine[1], mine[2], mine[3]
-    held = lax.ppermute(jnp.stack([fast_weights, momentum]), "seq", swap)
 
     reach = WINDOW // (2 * tokens)
     own_pair = mine[:2]
@@ -367,12 +434,10 @@
             token_product(key_hidden, outs),
         ]
     ).astype(jnp.bfloat16).reshape(3, half, rows, head_dim)
-    new_weights, new_momentum, applied = updated(total, held[0], held[1])
+    new_weights, new_momentum, applied = updated(total, fast_weights, momentum)
     asks, applied = lax.optimization_barrier((asks, applied))
     base = jnp.reshape((me // 2) * (2 * tokens), (1,)).astype(jnp.int32)
     att_normed = window_attention(base, asks, window)
-    owned = lax.ppermute(jnp.stack([new_weights, new_momentum]), "seq", swap)
-
     query_gate = row_product(asks, applied[0])
     query_up = row_product(asks, applied[1])
     query_hidden = (jax.nn.silu(query_gate) * query_up).astype(jnp.bfloat16)
@@ -390,7 +455,7 @@
     layer_out = jnp.concatenate(
         [jnp.where(first_core, stay, back), jnp.where(first_core, back, stay)], axis=1
     )
-    return (layer_out, owned[0], owned[1])
+    return (layer_out, new_weights, new_momentum)
 
 
 def solution(mesh):

time: 209 us -> 212 us (1.014)
  Pallas kernels: 119 us -> 154 us
  starting transfers between devices: 24.5 us -> 6.21 us
  waiting for transfers between devices: 25.6 us -> 12.3 us
  local copies, waits for them, and re-layouts: 13.1 us -> 16.9 us
  other arithmetic: 9.59 us -> 7.05 us
    pallas_call x1, Pallas kernels: 81.9 us -> 112 us  [updated(): pl.pallas_call(functools.partial(update_kernel, outer, inner), out_shape=...]
    ppermute x3 -> x0, starting transfers between devices: 18.8 us -> none  [the longest x1 11.3 us: per_device(): owned = lax.ppermute(jnp.stack([new_weights, new_momentum]), 'seq', swap)]
    ppermute x3 -> x0, waiting for transfers between devices: 15.1 us -> none  [the longest x1 15.1 us: per_device(): held16 = lax.ppermute(fast_weights.astype(jnp.bfloat16), 'seq', swap)]
    unnamed x33 -> x47, local copies, waits for them, and re-layouts: 3.02 us -> 9.59 us
    pallas_call x1, Pallas kernels: 28 us -> 32.9 us  [gathered(): pl.pallas_call(functools.partial(gather_kernel, outer, inner), out_shape=...]
    squeeze x2 -> x0, local copies, waits for them, and re-layouts: 2.78 us -> none  [the longest x1 1.92 us: per_device(): return (layer_out, owned[0], owned[1])]
  transfers between devices with their start and end apart: 7 -> 4, of which waited for: 2 -> 2; matrix products, arithmetic and copies ran while one was open for 13% -> 10% of each run, Pallas kernels for 57% -> 68%
where the time goes in v4:
time: 212 us
  Pallas kernels  154 us (73%)
  local copies, waits for them, and re-layouts  16.9 us (8%)
  matrix products  14.6 us (7%)
  waiting for transfers between devices  12.3 us (6%)
  other arithmetic  7.05 us (3%)
  starting transfers between devices  6.21 us (3%)
    pallas_call x1, Pallas kernels, updated(): pl.pallas_call(functools.partial(update_kernel, outer, inner), out_shape=...  112 us
    pallas_call x1, Pallas kernels, gathered(): pl.pallas_call(functools.partial(gather_kernel, outer, inner), out_shape=...  32.9 us
    ppermute x1, waiting for transfers between devices, per_device(): distant = lax.ppermute(own_pair, 'seq', ahead)  11 us
    unnamed x47, local copies, waits for them, and re-layouts  9.59 us
    pallas_call x1, Pallas kernels, window_attention(): pl.pallas_call(functools.partial(attention_kernel, tile, len(window)), ou...  9.1 us
    dot_general x4, matrix products, row_product(): lax.dot_general(left_side, right_side, (((1,), (1,)), ((), ())), preferre...  5.87 us
    dot_general x3, matrix products, token_product(): lax.dot_general(left_side, right_side, (((0,), (0,)), ((), ())), preferre...  4.44 us
    dot_general x1, matrix products, per_device(): jnp.dot(query_hidden, applied[2], preferred_element_type=jnp.float32)  4.27 us
  transfers between devices with their start and end apart: 4, of which 2 were waited for; matrix products, arithmetic and copies ran while one was open for 10% of the time, Pallas kernels for 68%

profile of v4, /device:TPU:1, one launch (start us, length us, event | category | flops | bytes accessed | tf_op | source)
XLA Modules:
  0.0 211.6 jit_solution(5566620728904889319)
XLA Ops:
  0.6 0.7 multiply_bitcast_fusion
  2.0 1.0 copy-done.13
  3.1 0.9 copy-done.18
  4.6 1.2 broadcast_select_fusion.3
  5.8 0.7 copy-done.11
  6.6 32.9 %shard_map.94 = bf16[3,16,40,640]{3,2,1,0:T(8,128)(2,1)S(1)} custom-call(bf16[3,40,640]{2,1,0:T(8,128)(2,1)S(1)} %convert_element_type.31.own), custom_call_target="tpu_custom_call" | custom-call | bytes 100000000 | tf_op jit(solution)/shard_map/pallas_call | solution.py:331
  39.8 1.5 copy-done.12
  41.3 1.6 broadcast_select_fusion.1
  43.1 0.8 convolution_bitcast_fusion.2
  43.9 2.0 collective-permute-start.1
  46.1 0.8 convolution_bitcast_fusion.1
  47.0 2.4 %multiply_convert_fusion.2 = (bf16[640,512]{0,1:T(8,128)(2,1)}, bf16[640,512]{0,1:T(8,128)(2,1)}, bf16[640,512]{0,1:T(8,128)(2,1)}) fusion(f32[640,512]{0,1:T(8,128)S(1)} %convolution_bitcast_fusion.2, f32[640,512]{0,1:T(8,128)S(1)} %convolution_bitcast_fusion.1, bf16[640,640]{1,0:T(8,128)(2,1)S(1)} %bitcast.79, bf16[1,512,640]{2,1,0:T(8,128)(2,1)S(1)} %get-tuple-element.18), kind=kOutput, calls=%fused_computation.21 | convolution fusion | flops 424345600 | bytes 6062080 | tf_op jit(solution)/shard_map/dot_general | solution.py:21
  49.4 2.2 %copy.17 = bf16[640,512]{1,0:T(8,128)(2,1)} copy(bf16[640,512]{0,1:T(8,128)(2,1)} %get-tuple-element.16) | data formatting | bytes 1310720 | tf_op jit(solution)/shard_map/convert_element_type | solution.py:426
  51.6 2.2 %copy.16 = bf16[640,512]{1,0:T(8,128)(2,1)} copy(bf16[640,512]{0,1:T(8,128)(2,1)} %get-tuple-element.17) | data formatting | bytes 1310720 | tf_op jit(solution)/shard_map/convert_element_type | solution.py:428
  53.8 2.2 %copy.15 = bf16[640,512]{1,0:T(8,128)(2,1)} copy(bf16[640,512]{0,1:T(8,128)(2,1)} %get-tuple-element.15) | data formatting | bytes 1310720 | tf_op jit(solution)/shard_map/convert_element_type | solution.py:427
  55.9 2.1 fusion.3
  58.1 1.7 fusion.4
  59.8 11.0 %collective-permute-done.1.refs_0_ = bf16[2,512,640]{2,1,0:T(8,128)(2,1)S(1)} collective-permute-done((bf16[2,512,640]{2,1,0:T(8,128)(2,1)S(1)}, bf16[2,512,640]{2,1,0:T(8,128)(2,1)S(1)}, u32[]{:S(2)}, u32[]{:S(2)}) %collective-permute-start.1) | collective-permute-done | bytes 1310752 | tf_op jit(solution)/shard_map/ppermute | solution.py:414
  70.8 1.2 broadcast_select_fusion
  72.0 1.6 collective-permute-start.2
  75.3 111.6 %shard_map.95 = (f32[3,40,640]{2,1,0:T(8,128)S(1)}, f32[3,40,640]{2,1,0:T(8,128)S(1)}, bf16[3,16,40,640]{3,2,1,0:T(8,128)(2,1)S(1)}) custom-call(bf16[3,16,40,640]{3,2,1,0:T(8,128)(2,1)S(1)} %pad_maximum_fusion.1.part, f32[3,40,640]{2,1,0:T(8,128)S(1)} %copy-done.1, f32[3,40,640]{2,1,0:T(8,128)S(1)} %copy-done.2), custom_call_target="tpu_custom_call" | custom-call | bytes 200000000 | tf_op jit(solution)/shard_map/pallas_call | solution.py:352
  186.9 0.8 copy-done.3
  187.7 0.7 copy-done.5
  188.4 1.4 copy-done.7
  189.8 1.8 fusion.9
  191.7 4.3 %multiply_reduce_fusion = (f32[512]{0:T(512)S(1)}, f32[512,640]{1,0:T(8,128)}) fusion(bf16[3,640,640]{2,1,0:T(8,128)(2,1)} %bitcast.72, bf16[512,640]{1,0:T(8,128)(2,1)S(1)} %get-tuple-element.9.q_ref, f32[512,640]{1,0:T(8,128)} %fusion.9), kind=kOutput, calls=%fused_computation.18 | convolution fusion | flops 841481728 | bytes 4917248 | tf_op jit(solution)/shard_map/dot_general | solution.py:444
  196.0 9.1 %shard_map.96 = f32[512,640]{1,0:T(8,128)S(1)} custom-call(s32[1]{0:T(128)} %bitcast.26.base_ref, bf16[512,640]{1,0:T(8,128)(2,1)S(1)} %get-tuple-element.9.q_ref, bf16[2,512,640]{2,1,0:T(8,128)(2,1)S(1)} %collective-permute-done.1.refs_0_, bf16[2,512,640]{2,1,0:T(8,128)(2,1)} %collective-permute-done.2.refs_1_, ...), custom_call_target="tpu_custom_call" | custom-call | flops 1677721600 | bytes 3932160 | tf_op jit(solution)/shard_map/pallas_call | solution.py:64
  205.4 2.5 %collective-permute-start.3 = (bf16[256,640]{1,0:T(8,128)(2,1)S(1)}, bf16[256,640]{1,0:T(8,128)(2,1)S(1)}, u32[]{:S(2)}, u32[]{:S(2)}) collective-permute-start(bf16[256,640]{1,0:T(8,128)(2,1)S(1)} %broadcast_select_fusion.7), channel_id=1, source_target_pairs={{0,1},{1,0},{2,3},{3,2},{4,5},{5,4},{6,7},{7,6},{8,9},{9,8},{10,11... | collective-permute-start | bytes 983048 | tf_op jit(solution)/shard_map/ppermute | solution.py:454
  207.9 1.3 collective-permute-done.3
  209.2 0.9 pad_maximum_fusion.3
  210.1 0.7 copy.21
  210.9 0.7 copy.22
  (56 shorter events, 4.1 us)
Async XLA Ops:
  1.9 1.1 copy-start.13
  3.0 1.1 copy-start.18
  3.0 1.3 copy-start.19
  4.6 1.9 copy-start.11
  4.6 2.0 copy-start
  6.5 33.3 %collective-permute-start = (bf16[4,256,640]{2,1,0:T(8,128)(2,1)}, bf16[4,256,640]{2,1,0:T(8,128)(2,1)}, u32[]{:S(2)}, u32[]{:S(2)}) collective-permute-start(bf16[4,256,640]{2,1,0:T(8,128)(2,1)} %broadcast_select_fusion.3), channel_id=1, source_target_pairs={{0,1},{1,0},{2,3},{3,2},{4,5},{5,4},{6,7},{7,6},{8,9},{9,8},{10,11... | collective-permute-start | bytes 3932168 | tf_op jit(solution)/shard_map/ppermute | solution.py:402
  6.6 32.9 %copy-start.21 = (f32[1280]{0:T(1024)S(1)}, f32[1280]{0:T(1024)}, u32[]{:S(2)}) copy-start(f32[1280]{0:T(1024)} %param.13) | copy-start | bytes 15364
  39.6 1.7 copy-start.12
  43.0 3.0 %copy-start.8 = (bf16[4,256,640]{2,1,0:T(8,128)(2,1)}, bf16[4,256,640]{2,1,0:T(8,128)(2,1)S(1)}, u32[]{:S(2)}) copy-start(bf16[4,256,640]{2,1,0:T(8,128)(2,1)S(1)} %get-tuple-element.13) | copy-start | bytes 3932164
  43.0 3.0 %copy-start.10 = (bf16[4,256,640]{2,1,0:T(8,128)(2,1)}, bf16[4,256,640]{2,1,0:T(8,128)(2,1)S(1)}, u32[]{:S(2)}) copy-start(bf16[4,256,640]{2,1,0:T(8,128)(2,1)S(1)} %get-tuple-element.14) | copy-start | bytes 3932164
  43.9 26.9 %collective-permute-start.1 = (bf16[2,512,640]{2,1,0:T(8,128)(2,1)S(1)}, bf16[2,512,640]{2,1,0:T(8,128)(2,1)S(1)}, u32[]{:S(2)}, u32[]{:S(2)}) collective-permute-start(bf16[2,512,640]{2,1,0:T(8,128)(2,1)S(1)} %pad_maximum_fusion.2.refs_2_), channel_id=1, source_target_pairs={{0,4},{1,5},{2,6},{3,7},{4,8},{5,9},{6,10},{7,11},{8,12},{9,13},{1... | collective-permute-start | bytes 3932168 | tf_op jit(solution)/shard_map/ppermute | solution.py:414
  46.1 0.9 copy-start.15
  55.9 2.1 %copy-start.9 = (bf16[4,256,640]{2,1,0:T(8,128)(2,1)S(1)}, bf16[4,256,640]{2,1,0:T(8,128)(2,1)}, u32[]{:S(2)}) copy-start(bf16[4,256,640]{2,1,0:T(8,128)(2,1)} %copy-done.8) | copy-start | bytes 3932164
  55.9 2.1 %copy-start.14 = (bf16[640,512]{1,0:T(8,128)(2,1)S(1)}, bf16[640,512]{1,0:T(8,128)(2,1)}, u32[]{:S(2)}) copy-start(bf16[640,512]{1,0:T(8,128)(2,1)} %copy.17) | copy-start | bytes 1966084
  59.7 13.8 %copy-start.16 = (bf16[1,512,640]{2,1,0:T(8,128)(2,1)S(1)}, bf16[1,512,640]{2,1,0:T(8,128)(2,1)}, u32[]{:S(2)}) copy-start(bf16[1,512,640]{2,1,0:T(8,128)(2,1)} %copy-done.15) | copy-start | bytes 1966084
  59.7 13.8 %copy-start.20 = (bf16[640,512]{1,0:T(8,128)(2,1)S(1)}, bf16[640,512]{1,0:T(8,128)(2,1)}, u32[]{:S(2)}) copy-start(bf16[640,512]{1,0:T(8,128)(2,1)} %copy.15) | copy-start | bytes 1966084
  72.0 124.0 %collective-permute-start.2 = (bf16[2,512,640]{2,1,0:T(8,128)(2,1)}, bf16[2,512,640]{2,1,0:T(8,128)(2,1)}, u32[]{:S(2)}, u32[]{:S(2)}) collective-permute-start(bf16[2,512,640]{2,1,0:T(8,128)(2,1)} %broadcast_select_fusion), channel_id=1, source_target_pairs={{0,2},{1,3},{2,0},{3,1},{4,6},{5,7},{6,4},{7,5},{8,10},{9,11},{10,... | collective-permute-start | bytes 3932168 | tf_op jit(solution)/shard_map/ppermute | solution.py:416
  74.3 1.0 copy-start.1
  74.3 1.1 copy-start.2
  186.9 0.8 copy-start.3
  187.7 0.7 copy-start.5
  188.4 1.4 copy-start.7
  195.9 9.1 %copy-start.17 = (f32[512,640]{1,0:T(8,128)S(1)}, f32[512,640]{1,0:T(8,128)}, u32[]{:S(2)}) copy-start(f32[512,640]{1,0:T(8,128)} %get-tuple-element.26) | copy-start | bytes 3932164
  205.4 3.8 %collective-permute-start.3 = (bf16[256,640]{1,0:T(8,128)(2,1)S(1)}, bf16[256,640]{1,0:T(8,128)(2,1)S(1)}, u32[]{:S(2)}, u32[]{:S(2)}) collective-permute-start(bf16[256,640]{1,0:T(8,128)(2,1)S(1)} %broadcast_select_fusion.7), channel_id=1, source_target_pairs={{0,1},{1,0},{2,3},{3,2},{4,5},{5,4},{6,7},{7,6},{8,9},{9,8},{10,11... | collective-permute-start | bytes 983048 | tf_op jit(solution)/shard_map/ppermute | solution.py:454
  207.9 2.3 %copy-start.6 = (f32[3,40,640]{2,1,0:T(8,128)S(1)}, f32[3,40,640]{2,1,0:T(8,128)}, u32[]{:S(2)}) copy-start(f32[3,40,640]{2,1,0:T(8,128)} %copy-done.5) | copy-start | bytes 921604
  209.2 1.6 copy-start.4

commit v5 on v4

--- a/solution.py
+++ b/solution.py
@@ -224,21 +224,12 @@
 
 
 def update_kernel(
-    outer, inner, part, own_weights, own_momentum, new_weights, new_momentum, out,
-    weights, momentum, fresh_weights, fresh_momentum, trade_sem,
+    outer, inner, part, weights, momentum, new_weights, new_momentum, out,
     near, mixed, sums, far, own16, near_send, near_recv, far_send, far_recv,
     local_sem, send_sem, recv_sem,
 ):
     a, b, device = place(outer, inner)
     greet(outer, inner, a, b, device)
-    take = trade(
-        outer,
-        inner,
-        [
-            (own_weights, weights, trade_sem.at[0], trade_sem.at[1]),
-            (own_momentum, momentum, trade_sem.at[2], trade_sem.at[3]),
-        ],
-    )
     steps = list(range(1, outer)) + [0]
     x, y, across = sides(b)
     near_copies = {}
@@ -291,25 +282,15 @@
     for j, one in enumerate(far_copies):
         one.wait_recv()
         total = total + far[j].astype(jnp.float32)
-    take()
     fast = weights[...]
     moment = 0.9 * momentum[...] + total
-    fresh_momentum[...] = moment
+    new_momentum[...] = moment
     moved = fast - moment
     keep_norm = jnp.sqrt(jnp.mean(fast * fast, axis=-1, keepdims=True))
     fresh = moved * keep_norm * lax.rsqrt(jnp.mean(moved * moved, axis=-1, keepdims=True) + 1e-06)
-    fresh_weights[...] = fresh
+    new_weights[...] = fresh
     own16[...] = fresh.astype(jnp.bfloat16)
-    give = trade(
-        outer,
-        inner,
-        [
-            (fresh_weights, new_weights, trade_sem.at[4], trade_sem.at[5]),
-            (fresh_momentum, new_momentum, trade_sem.at[6], trade_sem.at[7]),
-        ],
-    )
     gather(outer, inner, a, b, device, own16, out, local_sem, send_sem, recv_sem)
-    give()
     for one in far_copies:
         one.wait_send()
     for one in near_copies.values():
@@ -359,11 +340,6 @@
         in_specs=[vmem] * 3,
         out_specs=(vmem,) * 3,
         scratch_shapes=[
-            pltpu.VMEM(block, jnp.float32),
-            pltpu.VMEM(block, jnp.float32),
-            pltpu.VMEM(block, jnp.float32),
-            pltpu.VMEM(block, jnp.float32),
-            dma((8,)),
             pltpu.VMEM((3, outer) + block, jnp.bfloat16),
             pltpu.VMEM((outer,) + block, jnp.bfloat16),
             pltpu.VMEM((outer - 1,) + block, jnp.bfloat16),
@@ -392,7 +368,14 @@
     grad_scale = 1.0 / math.sqrt(tokens * size)
     pair = [(i, i ^ 1) for i in range(size)]
     half = size // 2
+    swap = []
+    for i in range(size):
+        head, m, core = i // half, (i % half) // 2, i % 2
+        swap.append((i, core * half + m * 2 + head))
     start_rows = gathered(fast_weights.astype(jnp.bfloat16))
+    state = jnp.stack([fast_weights, momentum])
+    state, start_rows = lax.optimization_barrier((state, start_rows))
+    held = lax.ppermute(state, "seq", swap)
 
     rates = jnp.repeat(step_rates.T, head_dim, axis=1)
     out_grad = (-grad_scale * rates * value_rows.astype(jnp.float32)).astype(jnp.bfloat16)
@@ -434,10 +417,12 @@
             token_product(key_hidden, outs),
         ]
     ).astype(jnp.bfloat16).reshape(3, half, rows, head_dim)
-    new_weights, new_momentum, applied = updated(total, fast_weights, momentum)
+    new_weights, new_momentum, applied = updated(total, held[0], held[1])
     asks, applied = lax.optimization_barrier((asks, applied))
     base = jnp.reshape((me // 2) * (2 * tokens), (1,)).astype(jnp.int32)
     att_normed = window_attention(base, asks, window)
+    owned = lax.ppermute(jnp.stack([new_weights, new_momentum]), "seq", swap)
+
     query_gate = row_product(asks, applied[0])
     query_up = row_product(asks, applied[1])
     query_hidden = (jax.nn.silu(query_gate) * query_up).astype(jnp.bfloat16)
@@ -455,7 +440,7 @@
     layer_out = jnp.concatenate(
         [jnp.where(first_core, stay, back), jnp.where(first_core, back, stay)], axis=1
     )
-    return (layer_out, new_weights, new_momentum)
+    return (layer_out, owned[0], owned[1])
 
 
 def solution(mesh):

time: 212 us -> 204 us (0.962); the launches traced: 212 us -> 200 us
  Pallas kernels: 154 us -> 128 us
  starting transfers between devices: 6.21 us -> 22.9 us
  local copies, waits for them, and re-layouts: 16.9 us -> 5.83 us
  waiting for transfers between devices: 12.3 us -> 21.7 us
  matrix products: 14.6 us -> 11 us
  other arithmetic: 7.05 us -> 9.75 us
    pallas_call x1, Pallas kernels: 112 us -> 86.2 us  [updated(): pl.pallas_call(functools.partial(update_kernel, outer, inner), out_shape=...]
    ppermute x0 -> x2, starting transfers between devices: none -> 17.2 us  [the longest x1 9.49 us: per_device(): held = lax.ppermute(state, 'seq', swap)]
    ppermute x0 -> x2, waiting for transfers between devices: none -> 10.3 us  [the longest x1 10.3 us: per_device(): held = lax.ppermute(state, 'seq', swap)]
    convert_element_type x3 -> x0, local copies, waits for them, and re-layouts: 6.53 us -> none  [the longest x1 2.18 us: per_device(): (hidden_grad * key_up * silu_slope(key_gate)).astype(jnp.bfloat16)]
    unnamed x47 -> x27, local copies, waits for them, and re-layouts: 9.59 us -> 4.39 us
    dot_general x3, matrix products: 4.44 us -> 2.05 us  [token_product(): lax.dot_general(left_side, right_side, (((0,), (0,)), ((), ())), preferre...]
  transfers between devices with their start and end apart: 4 -> 6, of which waited for: 2 -> 3; matrix products, arithmetic and copies ran while one was open for 10% -> 7% of each run, Pallas kernels for 68% -> 64%
where the time goes in v5:
time: 204 us; the launch traced here: 200 us
  Pallas kernels  128 us (63%)
  starting transfers between devices  22.9 us (11%)
  waiting for transfers between devices  21.7 us (11%)
  matrix products  11 us (5%)
  other arithmetic  9.75 us (5%)
  local copies, waits for them, and re-layouts  5.83 us (3%)
    pallas_call x1, Pallas kernels, updated(): pl.pallas_call(functools.partial(update_kernel, outer, inner), out_shape=...  86.2 us
    pallas_call x1, Pallas kernels, gathered(): pl.pallas_call(functools.partial(gather_kernel, outer, inner), out_shape=...  32.9 us
    ppermute x1, waiting for transfers between devices, per_device(): distant = lax.ppermute(own_pair, 'seq', ahead)  10.9 us
    ppermute x1, waiting for transfers between devices, per_device(): held = lax.ppermute(state, 'seq', swap)  10.3 us
    ppermute x1, starting transfers between devices, per_device(): held = lax.ppermute(state, 'seq', swap)  9.49 us
    pallas_call x1, Pallas kernels, window_attention(): pl.pallas_call(functools.partial(attention_kernel, tile, len(window)), ou...  9.07 us
    ppermute x1, starting transfers between devices, per_device(): owned = lax.ppermute(jnp.stack([new_weights, new_momentum]), 'seq', swap)  7.66 us
    dot_general x4, matrix products, row_product(): lax.dot_general(left_side, right_side, (((1,), (1,)), ((), ())), preferre...  4.55 us
  transfers between devices with their start and end apart: 6, of which 3 were waited for; matrix products, arithmetic and copies ran while one was open for 7% of the time, Pallas kernels for 64%

profile of v5, /device:TPU:1, one launch (start us, length us, event | category | flops | bytes accessed | tf_op | source)
XLA Modules:
  0.0 200.3 jit_solution(4749503065836709750)
XLA Ops:
  0.6 0.7 multiply_bitcast_fusion
  1.5 0.4 broadcast_in_dim.2
  2.0 1.0 copy-done.6
  3.1 0.9 copy-done.9
  4.6 1.2 broadcast_select_fusion.3
  5.9 0.7 copy-done.5
  6.6 32.9 %shard_map.94 = bf16[3,16,40,640]{3,2,1,0:T(8,128)(2,1)S(1)} custom-call(bf16[3,40,640]{2,1,0:T(8,128)(2,1)S(1)} %convert_element_type.31.own), custom_call_target="tpu_custom_call" | custom-call | bytes 100000000 | tf_op jit(solution)/shard_map/pallas_call | solution.py:312
  39.6 0.9 pad_maximum_fusion.4
  40.4 9.5 %collective-permute-start.1 = (f32[2,3,40,640]{3,2,1,0:T(8,128)}, f32[2,3,40,640]{3,2,1,0:T(8,128)S(1)}, u32[]{:S(2)}, u32[]{:S(2)}) collective-permute-start(f32[2,3,40,640]{3,2,1,0:T(8,128)} %pad_maximum_fusion.4), channel_id=1, source_target_pairs={{0,0},{1,16},{2,2},{3,18},{4,4},{5,20},{6,6},{7,22},{8,8},{9,24},{... | collective-permute-start | bytes 1843208 | tf_op jit(solution)/shard_map/ppermute | solution.py:378
  50.0 10.3 %collective-permute-done.1 = f32[2,3,40,640]{3,2,1,0:T(8,128)S(1)} collective-permute-done((f32[2,3,40,640]{3,2,1,0:T(8,128)}, f32[2,3,40,640]{3,2,1,0:T(8,128)S(1)}, u32[]{:S(2)}, u32[]{:S(2)}) %collective-permute-start.1) | collective-permute-done | bytes 614432 | tf_op jit(solution)/shard_map/ppermute | solution.py:378
  60.4 2.4 %broadcast_select_fusion.1 = (bf16[4,256,640]{2,1,0:T(8,128)(2,1)S(1)}, bf16[4,256,640]{2,1,0:T(8,128)(2,1)S(1)}) fusion(bf16[4,256,640]{2,1,0:T(8,128)(2,1)} %collective-permute-done, pred[]{:T(512)S(6)} %eq.9, bf16[4,256,1280]{2,1,0:T(8,128)(2,1)} %copy-done.5), kind=kLoop, calls=%fused_computation.23 | loop fusion | flops 1966080 | bytes 6553601 | tf_op jit(solution)/shard_map/jit(_where)/select_n | solution.py:387
  62.9 0.7 fusion.15
  63.6 2.0 collective-permute-start.2
  65.7 0.7 fusion.13
  66.4 1.3 multiply_convert_fusion.2
  67.7 0.7 fusion.3
  68.4 0.7 fusion.4
  69.1 10.9 %collective-permute-done.2.refs_0_ = bf16[2,512,640]{2,1,0:T(8,128)(2,1)S(1)} collective-permute-done((bf16[2,512,640]{2,1,0:T(8,128)(2,1)S(1)}, bf16[2,512,640]{2,1,0:T(8,128)(2,1)S(1)}, u32[]{:S(2)}, u32[]{:S(2)}) %collective-permute-start.2) | collective-permute-done | bytes 1310752 | tf_op jit(solution)/shard_map/ppermute | solution.py:397
  80.1 1.3 broadcast_select_fusion
  81.5 2.2 %collective-permute-start.3 = (bf16[2,512,640]{2,1,0:T(8,128)(2,1)}, bf16[2,512,640]{2,1,0:T(8,128)(2,1)}, u32[]{:S(2)}, u32[]{:S(2)}) collective-permute-start(bf16[2,512,640]{2,1,0:T(8,128)(2,1)} %broadcast_select_fusion), channel_id=1, source_target_pairs={{0,2},{1,3},{2,0},{3,1},{4,6},{5,7},{6,4},{7,5},{8,10},{9,11},{10,... | collective-permute-start | bytes 3932168 | tf_op jit(solution)/shard_map/ppermute | solution.py:399
  83.7 0.7 fusion.2
  84.7 86.2 %shard_map.95 = (f32[3,40,640]{2,1,0:T(8,128)S(1)}, f32[3,40,640]{2,1,0:T(8,128)S(1)}, bf16[3,16,40,640]{3,2,1,0:T(8,128)(2,1)S(1)}) custom-call(bf16[3,16,40,640]{3,2,1,0:T(8,128)(2,1)S(1)} %pad_maximum_fusion.1.part, f32[3,40,640]{2,1,0:T(8,128)S(1)} %get-tuple-element.29.weights, f32[3,40,640]{2,1,0:T(8,128)S(1)} %get-tuple-element.28.momentum), custom_call_target="tpu_custom_call" | custom-call | bytes 200000000 | tf_op jit(solution)/shard_map/pallas_call | solution.py:333
  171.0 1.0 pad_maximum_fusion.5
  171.9 7.7 %collective-permute-start.5 = (f32[2,3,40,640]{3,2,1,0:T(8,128)}, f32[2,3,40,640]{3,2,1,0:T(8,128)S(1)}, u32[]{:S(2)}, u32[]{:S(2)}) collective-permute-start(f32[2,3,40,640]{3,2,1,0:T(8,128)} %pad_maximum_fusion.5), channel_id=1, source_target_pairs={{0,0},{1,16},{2,2},{3,18},{4,4},{5,20},{6,6},{7,22},{8,8},{9,24},{... | collective-permute-start | bytes 1843208 | tf_op jit(solution)/shard_map/ppermute | solution.py:424
  179.6 1.8 fusion.9
  181.4 4.4 %multiply_reduce_fusion = (f32[512]{0:T(512)S(1)}, f32[512,640]{1,0:T(8,128)}) fusion(bf16[3,640,640]{2,1,0:T(8,128)(2,1)} %bitcast.89, bf16[512,640]{1,0:T(8,128)(2,1)S(1)} %get-tuple-element.13.q_ref, f32[512,640]{1,0:T(8,128)} %fusion.9), kind=kOutput, calls=%fused_computation.15 | convolution fusion | flops 841481728 | bytes 4917248 | tf_op jit(solution)/shard_map/dot_general | solution.py:429
  185.9 1.3 copy-done.3
  187.2 9.1 %shard_map.96 = f32[512,640]{1,0:T(8,128)S(1)} custom-call(s32[1]{0:T(128)} %bitcast.28.base_ref, bf16[512,640]{1,0:T(8,128)(2,1)S(1)} %get-tuple-element.13.q_ref, bf16[2,512,640]{2,1,0:T(8,128)(2,1)S(1)} %copy-done.3, bf16[2,512,640]{2,1,0:T(8,128)(2,1)} %collective-permute-done.3.refs_1_, bf16[2,512,640]{2,1,0:T(8,128)(2,1)S(1)} %copy-done.1), custom_call_target="tpu_custom_call" | custom-call | flops 1677721600 | bytes 3932160 | tf_op jit(solution)/shard_map/pallas_call | solution.py:64
  196.6 1.5 collective-permute-start.4
  198.1 0.9 slice_bitcast_fusion
  199.0 0.4 collective-permute-done.4
  199.5 0.9 pad_maximum_fusion.3
  (40 shorter events, 2.1 us)
Async XLA Ops:
  1.9 1.1 copy-start.6
  3.0 1.1 copy-start.9
  3.0 1.3 copy-start.10
  4.6 1.9 copy-start.5
  4.6 2.0 copy-start.8
  6.5 53.9 %collective-permute-start = (bf16[4,256,640]{2,1,0:T(8,128)(2,1)}, bf16[4,256,640]{2,1,0:T(8,128)(2,1)}, u32[]{:S(2)}, u32[]{:S(2)}) collective-permute-start(bf16[4,256,640]{2,1,0:T(8,128)(2,1)} %broadcast_select_fusion.3), channel_id=1, source_target_pairs={{0,1},{1,0},{2,3},{3,2},{4,5},{5,4},{6,7},{7,6},{8,9},{9,8},{10,11... | collective-permute-start | bytes 3932168 | tf_op jit(solution)/shard_map/ppermute | solution.py:385
  6.6 32.9 %copy-start.11 = (f32[3,40,640]{2,1,0:T(8,128)S(1)}, f32[3,40,640]{2,1,0:T(8,128)}, u32[]{:S(2)}) copy-start(f32[3,40,640]{2,1,0:T(8,128)} %param.12) | copy-start | bytes 921604
  6.6 43.4 %copy-start.12 = (f32[1280]{0:T(1024)S(1)}, f32[1280]{0:T(1024)}, u32[]{:S(2)}) copy-start(f32[1280]{0:T(1024)} %param.13) | copy-start | bytes 15364
  40.4 19.9 %collective-permute-start.1 = (f32[2,3,40,640]{3,2,1,0:T(8,128)}, f32[2,3,40,640]{3,2,1,0:T(8,128)S(1)}, u32[]{:S(2)}, u32[]{:S(2)}) collective-permute-start(f32[2,3,40,640]{3,2,1,0:T(8,128)} %pad_maximum_fusion.4), channel_id=1, source_target_pairs={{0,0},{1,16},{2,2},{3,18},{4,4},{5,20},{6,6},{7,22},{8,8},{9,24},{... | collective-permute-start | bytes 1843208 | tf_op jit(solution)/shard_map/ppermute | solution.py:378
  62.9 17.1 %copy-start = (bf16[2,512,640]{2,1,0:T(8,128)(2,1)}, bf16[2,512,640]{2,1,0:T(8,128)(2,1)S(1)}, u32[]{:S(2)}) copy-start(bf16[2,512,640]{2,1,0:T(8,128)(2,1)S(1)} %pad_maximum_fusion.2.refs_2_) | copy-start | bytes 3932164
  63.6 16.4 %collective-permute-start.2 = (bf16[2,512,640]{2,1,0:T(8,128)(2,1)S(1)}, bf16[2,512,640]{2,1,0:T(8,128)(2,1)S(1)}, u32[]{:S(2)}, u32[]{:S(2)}) collective-permute-start(bf16[2,512,640]{2,1,0:T(8,128)(2,1)S(1)} %pad_maximum_fusion.2.refs_2_), channel_id=1, source_target_pairs={{0,4},{1,5},{2,6},{3,7},{4,8},{5,9},{6,10},{7,11},{8,12},{9,13},{1... | collective-permute-start | bytes 3932168 | tf_op jit(solution)/shard_map/ppermute | solution.py:397
  80.1 1.5 copy-start.2
  81.5 104.3 %collective-permute-start.3 = (bf16[2,512,640]{2,1,0:T(8,128)(2,1)}, bf16[2,512,640]{2,1,0:T(8,128)(2,1)}, u32[]{:S(2)}, u32[]{:S(2)}) collective-permute-start(bf16[2,512,640]{2,1,0:T(8,128)(2,1)} %broadcast_select_fusion), channel_id=1, source_target_pairs={{0,2},{1,3},{2,0},{3,1},{4,6},{5,7},{6,4},{7,5},{8,10},{9,11},{10,... | collective-permute-start | bytes 3932168 | tf_op jit(solution)/shard_map/ppermute | solution.py:399
  170.9 8.6 %copy-start.4 = (bf16[3,16,40,640]{3,2,1,0:T(8,128)(2,1)}, bf16[3,16,40,640]{3,2,1,0:T(8,128)(2,1)S(1)}, u32[]{:S(2)}) copy-start(bf16[3,16,40,640]{3,2,1,0:T(8,128)(2,1)S(1)} %get-tuple-element.12) | copy-start | bytes 7372804
  171.9 26.2 %collective-permute-start.5 = (f32[2,3,40,640]{3,2,1,0:T(8,128)}, f32[2,3,40,640]{3,2,1,0:T(8,128)S(1)}, u32[]{:S(2)}, u32[]{:S(2)}) collective-permute-start(f32[2,3,40,640]{3,2,1,0:T(8,128)} %pad_maximum_fusion.5), channel_id=1, source_target_pairs={{0,0},{1,16},{2,2},{3,18},{4,4},{5,20},{6,6},{7,22},{8,8},{9,24},{... | collective-permute-start | bytes 1843208 | tf_op jit(solution)/shard_map/ppermute | solution.py:424
  181.4 4.4 %copy-start.1 = (bf16[2,512,640]{2,1,0:T(8,128)(2,1)S(1)}, bf16[2,512,640]{2,1,0:T(8,128)(2,1)}, u32[]{:S(2)}) copy-start(bf16[2,512,640]{2,1,0:T(8,128)(2,1)} %copy-done) | copy-start | bytes 3932164
  185.9 1.3 copy-start.3
  187.2 9.1 %copy-start.7 = (f32[512,640]{1,0:T(8,128)S(1)}, f32[512,640]{1,0:T(8,128)}, u32[]{:S(2)}) copy-start(f32[512,640]{1,0:T(8,128)} %get-tuple-element.31) | copy-start | bytes 3932164
  196.6 2.8 %collective-permute-start.4 = (bf16[256,640]{1,0:T(8,128)(2,1)S(1)}, bf16[256,640]{1,0:T(8,128)(2,1)S(1)}, u32[]{:S(2)}, u32[]{:S(2)}) collective-permute-start(bf16[256,640]{1,0:T(8,128)(2,1)S(1)} %broadcast_select_fusion.7), channel_id=1, source_target_pairs={{0,1},{1,0},{2,3},{3,2},{4,5},{5,4},{6,7},{7,6},{8,9},{9,8},{10,11... | collective-permute-start | bytes 983048 | tf_op jit(solution)/shard_map/ppermute | solution.py:439

commit v6 on v5

--- a/solution.py
+++ b/solution.py
@@ -372,10 +372,6 @@
     for i in range(size):
         head, m, core = i // half, (i % half) // 2, i % 2
         swap.append((i, core * half + m * 2 + head))
-    start_rows = gathered(fast_weights.astype(jnp.bfloat16))
-    state = jnp.stack([fast_weights, momentum])
-    state, start_rows = lax.optimization_barrier((state, start_rows))
-    held = lax.ppermute(state, "seq", swap)
 
     rates = jnp.repeat(step_rates.T, head_dim, axis=1)
     out_grad = (-grad_scale * rates * value_rows.astype(jnp.float32)).astype(jnp.bfloat16)
@@ -388,13 +384,16 @@
     )
     keys, values, outs, asks = mine[0], mine[1], mine[2], mine[3]
 
+    state = jnp.stack([fast_weights, momentum])
     reach = WINDOW // (2 * tokens)
+    start_rows = gathered(fast_weights.astype(jnp.bfloat16))
     own_pair = mine[:2]
     window = [own_pair]
     if reach == 2:
         ahead = [(i, i + 4) for i in range(size - 4)]
         beside = [(i, i ^ 2) for i in range(size)]
         distant = lax.ppermute(own_pair, "seq", ahead)
+        state, distant = lax.optimization_barrier((state, distant))
         even_chip = (me // 2) % 2 == 0
         close = lax.ppermute(jnp.where(even_chip, own_pair, distant), "seq", beside)
         window = [distant, close, own_pair]
@@ -403,6 +402,7 @@
             route = [(i, i + 2 * hop) for i in range(size - 2 * hop)]
             window.insert(0, lax.ppermute(own_pair, "seq", route))
 
+    held = lax.ppermute(state, "seq", swap)
     key_gate = row_product(keys, start_rows[0])
     key_up = row_product(keys, start_rows[1])
     hidden_grad = row_product(outs, start_rows[2])

time: 204 us -> 206 us (level)
  Pallas kernels: 128 us -> 120 us
  local copies, waits for them, and re-layouts: 5.83 us -> 13.8 us
  starting transfers between devices: 22.9 us -> 28.3 us
  waiting for transfers between devices: 21.7 us -> 16.3 us
  matrix products: 11 us -> 14.7 us
    pallas_call x1, Pallas kernels: 86.2 us -> 78 us  [updated(): pl.pallas_call(functools.partial(update_kernel, outer, inner), out_shape=...]
    convert_element_type x0 -> x3, local copies, waits for them, and re-layouts: none -> 6.53 us  [the longest x1 2.19 us: per_device(): up_grad = (hidden_grad * jax.nn.silu(key_gate)).astype(jnp.bfloat16)]
    ppermute x1, waiting for transfers between devices: 10.3 us -> 5.33 us  [per_device(): held = lax.ppermute(state, 'seq', swap)]
    ppermute x1, starting transfers between devices: 1.55 us -> 4.56 us  [per_device(): back = lax.ppermute(jnp.where(first_core, late, early), 'seq', pair)]
    ppermute x1, starting transfers between devices: 7.66 us -> 10.3 us  [per_device(): owned = lax.ppermute(jnp.stack([new_weights, new_momentum]), 'seq', swap)]
    dot_general x3, matrix products: 2.05 us -> 4.59 us  [token_product(): lax.dot_general(left_side, right_side, (((0,), (0,)), ((), ())), preferre...]
    unnamed x27 -> x37, local copies, waits for them, and re-layouts: 4.39 us -> 4.5 us
  transfers between devices with their start and end apart: 6 -> 6, of which waited for: 3 -> 2; matrix products, arithmetic and copies ran while one was open for 7% -> 13% of each run, Pallas kernels for 64% -> 59%
where the time goes in v6:
time: 206 us; the launch traced here: 203 us
  Pallas kernels  120 us (58%)
  starting transfers between devices  28.3 us (14%)
  waiting for transfers between devices  16.3 us (8%)
  matrix products  14.7 us (7%)
  local copies, waits for them, and re-layouts  13.8 us (7%)
  other arithmetic  8.85 us (4%)
    pallas_call x1, Pallas kernels, updated(): pl.pallas_call(functools.partial(update_kernel, outer, inner), out_shape=...  78 us
    pallas_call x1, Pallas kernels, gathered(): pl.pallas_call(functools.partial(gather_kernel, outer, inner), out_shape=...  32.9 us
    ppermute x1, starting transfers between devices, per_device(): held = lax.ppermute(state, 'seq', swap)  11.1 us
    ppermute x1, waiting for transfers between devices, per_device(): distant = lax.ppermute(own_pair, 'seq', ahead)  10.9 us
    ppermute x1, starting transfers between devices, per_device(): owned = lax.ppermute(jnp.stack([new_weights, new_momentum]), 'seq', swap)  10.3 us
    pallas_call x1, Pallas kernels, window_attention(): pl.pallas_call(functools.partial(attention_kernel, tile, len(window)), ou...  9.09 us
    dot_general x4, matrix products, row_product(): lax.dot_general(left_side, right_side, (((1,), (1,)), ((), ())), preferre...  5.84 us
    ppermute x1, waiting for transfers between devices, per_device(): held = lax.ppermute(state, 'seq', swap)  5.33 us
  transfers between devices with their start and end apart: 6, of which 2 were waited for; matrix products, arithmetic and copies ran while one was open for 13% of the time, Pallas kernels for 59%

profile of v6, /device:TPU:1, one launch (start us, length us, event | category | flops | bytes accessed | tf_op | source)
XLA Modules:
  0.0 202.9 jit_solution(7107533223037289014)
XLA Ops:
  0.6 0.7 multiply_bitcast_fusion
  2.0 1.0 copy-done.6
  3.1 0.9 copy-done.12
  4.6 1.2 broadcast_select_fusion.3
  5.8 0.7 copy-done.4
  6.6 32.9 %shard_map.94 = bf16[3,16,40,640]{3,2,1,0:T(8,128)(2,1)S(1)} custom-call(bf16[3,40,640]{2,1,0:T(8,128)(2,1)S(1)} %convert_element_type.31.own), custom_call_target="tpu_custom_call" | custom-call | bytes 100000000 | tf_op jit(solution)/shard_map/pallas_call | solution.py:312
  39.6 0.9 pad_maximum_fusion.4
  40.7 1.5 copy-done.5
  42.2 1.6 broadcast_select_fusion.1
  44.0 0.8 convolution_bitcast_fusion.2
  44.8 2.1 %collective-permute-start.1 = (bf16[2,512,640]{2,1,0:T(8,128)(2,1)S(1)}, bf16[2,512,640]{2,1,0:T(8,128)(2,1)S(1)}, u32[]{:S(2)}, u32[]{:S(2)}) collective-permute-start(bf16[2,512,640]{2,1,0:T(8,128)(2,1)S(1)} %pad_maximum_fusion.2.refs_2_), channel_id=1, source_target_pairs={{0,4},{1,5},{2,6},{3,7},{4,8},{5,9},{6,10},{7,11},{8,12},{9,13},{1... | collective-permute-start | bytes 3932168 | tf_op jit(solution)/shard_map/ppermute | solution.py:395
  47.0 0.8 convolution_bitcast_fusion.1
  47.8 2.4 %multiply_convert_fusion.2 = (bf16[640,512]{0,1:T(8,128)(2,1)}, bf16[640,512]{0,1:T(8,128)(2,1)}, bf16[640,512]{0,1:T(8,128)(2,1)}) fusion(f32[640,512]{0,1:T(8,128)S(1)} %convolution_bitcast_fusion.2, f32[640,512]{0,1:T(8,128)S(1)} %convolution_bitcast_fusion.1, bf16[640,640]{1,0:T(8,128)(2,1)S(1)} %bitcast.94, bf16[1,512,640]{2,1,0:T(8,128)(2,1)S(1)} %get-tuple-element.22), kind=kOutput, calls=%fused_computation.21 | convolution fusion | flops 424345600 | bytes 6062080 | tf_op jit(solution)/shard_map/dot_general | solution.py:21
  50.3 2.2 %copy.17 = bf16[640,512]{1,0:T(8,128)(2,1)} copy(bf16[640,512]{0,1:T(8,128)(2,1)} %get-tuple-element.20) | data formatting | bytes 1310720 | tf_op jit(solution)/shard_map/convert_element_type | solution.py:409
  52.4 2.2 %copy.16 = bf16[640,512]{1,0:T(8,128)(2,1)} copy(bf16[640,512]{0,1:T(8,128)(2,1)} %get-tuple-element.21) | data formatting | bytes 1310720 | tf_op jit(solution)/shard_map/convert_element_type | solution.py:411
  54.6 2.2 %copy.15 = bf16[640,512]{1,0:T(8,128)(2,1)} copy(bf16[640,512]{0,1:T(8,128)(2,1)} %get-tuple-element.19) | data formatting | bytes 1310720 | tf_op jit(solution)/shard_map/convert_element_type | solution.py:410
  56.8 2.1 %fusion.3 = bf16[1,16,40,640]{3,2,1,0:T(8,128)(2,1)S(1)} fusion(bf16[16,40,512]{2,1,0:T(8,128)(2,1)} %bitcast.98, bf16[1,512,640]{2,1,0:T(8,128)(2,1)} %copy-done.8), kind=kOutput, calls=%fused_computation.31 | convolution fusion | flops 419840000 | bytes 2129920 | tf_op jit(solution)/shard_map/dot_general | solution.py:27
  59.0 1.8 fusion.4
  60.8 10.9 %collective-permute-done.1.refs_0_ = bf16[2,512,640]{2,1,0:T(8,128)(2,1)S(1)} collective-permute-done((bf16[2,512,640]{2,1,0:T(8,128)(2,1)S(1)}, bf16[2,512,640]{2,1,0:T(8,128)(2,1)S(1)}, u32[]{:S(2)}, u32[]{:S(2)}) %collective-permute-start.1) | collective-permute-done | bytes 1310752 | tf_op jit(solution)/shard_map/ppermute | solution.py:395
  71.7 11.1 %collective-permute-start.2 = (f32[2,3,40,640]{3,2,1,0:T(8,128)S(1)}, f32[2,3,40,640]{3,2,1,0:T(8,128)S(1)}, u32[]{:S(2)}, u32[]{:S(2)}) collective-permute-start(f32[2,3,40,640]{3,2,1,0:T(8,128)S(1)} %copy-done.15), channel_id=1, source_target_pairs={{0,0},{1,16},{2,2},{3,18},{4,4},{5,20},{6,6},{7,22},{8,8},{9,24},{... | collective-permute-start | bytes 1843208 | tf_op jit(solution)/shard_map/ppermute | solution.py:405
  82.8 0.7 fusion.2
  83.9 1.2 broadcast_select_fusion
  85.3 5.3 %collective-permute-done.2 = f32[2,3,40,640]{3,2,1,0:T(8,128)S(1)} collective-permute-done((f32[2,3,40,640]{3,2,1,0:T(8,128)S(1)}, f32[2,3,40,640]{3,2,1,0:T(8,128)S(1)}, u32[]{:S(2)}, u32[]{:S(2)}) %collective-permute-start.2) | collective-permute-done | bytes 614432 | tf_op jit(solution)/shard_map/ppermute | solution.py:405
  90.7 78.0 %shard_map.95 = (f32[3,40,640]{2,1,0:T(8,128)S(1)}, f32[3,40,640]{2,1,0:T(8,128)S(1)}, bf16[3,16,40,640]{3,2,1,0:T(8,128)(2,1)S(1)}) custom-call(bf16[3,16,40,640]{3,2,1,0:T(8,128)(2,1)S(1)} %pad_maximum_fusion.1.part, f32[3,40,640]{2,1,0:T(8,128)S(1)} %get-tuple-element.32.weights, f32[3,40,640]{2,1,0:T(8,128)S(1)} %get-tuple-element.31.momentum), custom_call_target="tpu_custom_call" | custom-call | bytes 200000000 | tf_op jit(solution)/shard_map/pallas_call | solution.py:333
  168.7 0.9 pad_maximum_fusion.5
  169.6 10.3 %collective-permute-start.5 = (f32[2,3,40,640]{3,2,1,0:T(8,128)}, f32[2,3,40,640]{3,2,1,0:T(8,128)}, u32[]{:S(2)}, u32[]{:S(2)}) collective-permute-start(f32[2,3,40,640]{3,2,1,0:T(8,128)} %pad_maximum_fusion.5), channel_id=1, source_target_pairs={{0,0},{1,16},{2,2},{3,18},{4,4},{5,20},{6,6},{7,22},{8,8},{9,24},{... | collective-permute-start | bytes 1843208 | tf_op jit(solution)/shard_map/ppermute | solution.py:424
  179.9 1.8 fusion.9
  181.8 4.3 %multiply_reduce_fusion = (f32[512]{0:T(512)S(1)}, f32[512,640]{1,0:T(8,128)}) fusion(bf16[3,640,640]{2,1,0:T(8,128)(2,1)} %bitcast.86, bf16[512,640]{1,0:T(8,128)(2,1)S(1)} %get-tuple-element.12.q_ref, f32[512,640]{1,0:T(8,128)} %fusion.9), kind=kOutput, calls=%fused_computation.18 | convolution fusion | flops 841481728 | bytes 4917248 | tf_op jit(solution)/shard_map/dot_general | solution.py:429
  186.0 9.1 %shard_map.96 = f32[512,640]{1,0:T(8,128)S(1)} custom-call(s32[1]{0:T(128)} %bitcast.30.base_ref, bf16[512,640]{1,0:T(8,128)(2,1)S(1)} %get-tuple-element.12.q_ref, bf16[2,512,640]{2,1,0:T(8,128)(2,1)S(1)} %collective-permute-done.1.refs_0_, bf16[2,512,640]{2,1,0:T(8,128)(2,1)} %collective-permute-done.3.refs_1_, ...), custom_call_target="tpu_custom_call" | custom-call | flops 1677721600 | bytes 3932160 | tf_op jit(solution)/shard_map/pallas_call | solution.py:64
  195.4 4.6 %collective-permute-start.4 = (bf16[256,640]{1,0:T(8,128)(2,1)S(1)}, bf16[256,640]{1,0:T(8,128)(2,1)S(1)}, u32[]{:S(2)}, u32[]{:S(2)}) collective-permute-start(bf16[256,640]{1,0:T(8,128)(2,1)S(1)} %broadcast_select_fusion.7), channel_id=1, source_target_pairs={{0,1},{1,0},{2,3},{3,2},{4,5},{5,4},{6,7},{7,6},{8,9},{9,8},{10,11... | collective-permute-start | bytes 983048 | tf_op jit(solution)/shard_map/ppermute | solution.py:439
  200.0 1.9 slice_bitcast_fusion
  202.0 0.9 pad_maximum_fusion.3
  (54 shorter events, 2.9 us)
Async XLA Ops:
  1.9 1.1 copy-start.6
  3.0 1.1 copy-start.12
  3.0 1.3 copy-start.13
  4.6 1.9 copy-start.4
  4.6 2.0 copy-start.11
  6.5 34.2 %collective-permute-start = (bf16[4,256,640]{2,1,0:T(8,128)(2,1)}, bf16[4,256,640]{2,1,0:T(8,128)(2,1)}, u32[]{:S(2)}, u32[]{:S(2)}) collective-permute-start(bf16[4,256,640]{2,1,0:T(8,128)(2,1)} %broadcast_select_fusion.3), channel_id=1, source_target_pairs={{0,1},{1,0},{2,3},{3,2},{4,5},{5,4},{6,7},{7,6},{8,9},{9,8},{10,11... | collective-permute-start | bytes 3932168 | tf_op jit(solution)/shard_map/ppermute | solution.py:381
  6.6 33.0 %copy-start.16 = (f32[3,40,640]{2,1,0:T(8,128)S(1)}, f32[3,40,640]{2,1,0:T(8,128)}, u32[]{:S(2)}) copy-start(f32[3,40,640]{2,1,0:T(8,128)} %param.12) | copy-start | bytes 921604
  6.6 33.8 %copy-start.17 = (f32[1280]{0:T(1024)S(1)}, f32[1280]{0:T(1024)}, u32[]{:S(2)}) copy-start(f32[1280]{0:T(1024)} %param.13) | copy-start | bytes 15364
  40.5 1.7 copy-start.5
  43.9 3.0 %copy-start.1 = (bf16[4,256,640]{2,1,0:T(8,128)(2,1)}, bf16[4,256,640]{2,1,0:T(8,128)(2,1)S(1)}, u32[]{:S(2)}) copy-start(bf16[4,256,640]{2,1,0:T(8,128)(2,1)S(1)} %get-tuple-element.17) | copy-start | bytes 3932164
  43.9 3.0 %copy-start.3 = (bf16[4,256,640]{2,1,0:T(8,128)(2,1)}, bf16[4,256,640]{2,1,0:T(8,128)(2,1)S(1)}, u32[]{:S(2)}) copy-start(bf16[4,256,640]{2,1,0:T(8,128)(2,1)S(1)} %get-tuple-element.18) | copy-start | bytes 3932164
  44.8 26.9 %collective-permute-start.1 = (bf16[2,512,640]{2,1,0:T(8,128)(2,1)S(1)}, bf16[2,512,640]{2,1,0:T(8,128)(2,1)S(1)}, u32[]{:S(2)}, u32[]{:S(2)}) collective-permute-start(bf16[2,512,640]{2,1,0:T(8,128)(2,1)S(1)} %pad_maximum_fusion.2.refs_2_), channel_id=1, source_target_pairs={{0,4},{1,5},{2,6},{3,7},{4,8},{5,9},{6,10},{7,11},{8,12},{9,13},{1... | collective-permute-start | bytes 3932168 | tf_op jit(solution)/shard_map/ppermute | solution.py:395
  47.0 0.8 copy-start.8
  56.8 2.1 %copy-start.2 = (bf16[4,256,640]{2,1,0:T(8,128)(2,1)S(1)}, bf16[4,256,640]{2,1,0:T(8,128)(2,1)}, u32[]{:S(2)}) copy-start(bf16[4,256,640]{2,1,0:T(8,128)(2,1)} %copy-done.1) | copy-start | bytes 3932164
  56.8 2.1 %copy-start.7 = (bf16[640,512]{1,0:T(8,128)(2,1)S(1)}, bf16[640,512]{1,0:T(8,128)(2,1)}, u32[]{:S(2)}) copy-start(bf16[640,512]{1,0:T(8,128)(2,1)} %copy.17) | copy-start | bytes 1966084
  58.9 12.8 %copy-start.15 = (f32[2,3,40,640]{3,2,1,0:T(8,128)S(1)}, f32[2,3,40,640]{3,2,1,0:T(8,128)}, u32[]{:S(2)}) copy-start(f32[2,3,40,640]{3,2,1,0:T(8,128)} %pad_maximum_fusion.4) | copy-start | bytes 1843204
  59.0 23.9 %copy-start.9 = (bf16[1,512,640]{2,1,0:T(8,128)(2,1)S(1)}, bf16[1,512,640]{2,1,0:T(8,128)(2,1)}, u32[]{:S(2)}) copy-start(bf16[1,512,640]{2,1,0:T(8,128)(2,1)} %copy-done.8) | copy-start | bytes 1966084
  59.0 23.9 %copy-start.14 = (bf16[640,512]{1,0:T(8,128)(2,1)S(1)}, bf16[640,512]{1,0:T(8,128)(2,1)}, u32[]{:S(2)}) copy-start(bf16[640,512]{1,0:T(8,128)(2,1)} %copy.15) | copy-start | bytes 1966084
  71.7 18.9 %collective-permute-start.2 = (f32[2,3,40,640]{3,2,1,0:T(8,128)S(1)}, f32[2,3,40,640]{3,2,1,0:T(8,128)S(1)}, u32[]{:S(2)}, u32[]{:S(2)}) collective-permute-start(f32[2,3,40,640]{3,2,1,0:T(8,128)S(1)} %copy-done.15), channel_id=1, source_target_pairs={{0,0},{1,16},{2,2},{3,18},{4,4},{5,20},{6,6},{7,22},{8,8},{9,24},{... | collective-permute-start | bytes 1843208 | tf_op jit(solution)/shard_map/ppermute | solution.py:405
  85.1 101.0 %collective-permute-start.3 = (bf16[2,512,640]{2,1,0:T(8,128)(2,1)}, bf16[2,512,640]{2,1,0:T(8,128)(2,1)}, u32[]{:S(2)}, u32[]{:S(2)}) collective-permute-start(bf16[2,512,640]{2,1,0:T(8,128)(2,1)} %broadcast_select_fusion), channel_id=1, source_target_pairs={{0,2},{1,3},{2,0},{3,1},{4,6},{5,7},{6,4},{7,5},{8,10},{9,11},{10,... | collective-permute-start | bytes 3932168 | tf_op jit(solution)/shard_map/ppermute | solution.py:398
  168.7 11.3 %copy-start = (bf16[3,16,40,640]{3,2,1,0:T(8,128)(2,1)}, bf16[3,16,40,640]{3,2,1,0:T(8,128)(2,1)S(1)}, u32[]{:S(2)}) copy-start(bf16[3,16,40,640]{3,2,1,0:T(8,128)(2,1)S(1)} %get-tuple-element.11) | copy-start | bytes 7372804
  169.6 30.4 %collective-permute-start.5 = (f32[2,3,40,640]{3,2,1,0:T(8,128)}, f32[2,3,40,640]{3,2,1,0:T(8,128)}, u32[]{:S(2)}, u32[]{:S(2)}) collective-permute-start(f32[2,3,40,640]{3,2,1,0:T(8,128)} %pad_maximum_fusion.5), channel_id=1, source_target_pairs={{0,0},{1,16},{2,2},{3,18},{4,4},{5,20},{6,6},{7,22},{8,8},{9,24},{... | collective-permute-start | bytes 1843208 | tf_op jit(solution)/shard_map/ppermute | solution.py:424
  186.0 9.1 %copy-start.10 = (f32[512,640]{1,0:T(8,128)S(1)}, f32[512,640]{1,0:T(8,128)}, u32[]{:S(2)}) copy-start(f32[512,640]{1,0:T(8,128)} %get-tuple-element.34) | copy-start | bytes 3932164
  195.4 6.5 %collective-permute-start.4 = (bf16[256,640]{1,0:T(8,128)(2,1)S(1)}, bf16[256,640]{1,0:T(8,128)(2,1)S(1)}, u32[]{:S(2)}, u32[]{:S(2)}) collective-permute-start(bf16[256,640]{1,0:T(8,128)(2,1)S(1)} %broadcast_select_fusion.7), channel_id=1, source_target_pairs={{0,1},{1,0},{2,3},{3,2},{4,5},{5,4},{6,7},{7,6},{8,9},{9,8},{10,11... | collective-permute-start | bytes 983048 | tf_op jit(solution)/shard_map/ppermute | solution.py:439
